TPU v7x, 128 devices: a whole 4x4x4 slice. The times are simulated.
128 devices in a mesh: pipe: 8 (over x, core), expert: 16 (over z, y).
Axes of the slice: x: 4, y: 4, z: 4, core: 2. Of those that a mesh axis runs over, the one named last changes fastest.
Arguments:
- activations: bfloat16 [1, 2048, 2048], P(None, 'expert'), may hold values from -6 to 6
- norm_gain: bfloat16 [8, 2048], P('pipe'), may hold values from 0.25 to 1.75
- w_gate: bfloat16 [8, 16, 2048, 768], P('pipe', 'expert'), may hold values from -0.125 to 0.125
- w_up: bfloat16 [8, 16, 2048, 768], P('pipe', 'expert'), may hold values from -0.125 to 0.125
- w_down: bfloat16 [8, 16, 768, 2048], P('pipe', 'expert'), may hold values from -0.21875 to 0.21875
- routes: int32 [8, 1, 64, 2], P('pipe', None, 'expert'), may hold values from 0 to 15, as said below
- gate_scores: float32 [8, 1, 64, 2], P('pipe', None, 'expert'), may hold values from 0.25 to 4
Outputs:
- section_out: bfloat16 [8, 1, 2048, 2048], P('pipe', None, 'expert')
Inputs may be any that keep to these rules, and one draw needn't show every extreme that they name: `routes`: each entry names an expert. The 2 experts of one block differ. Among the 4 blocks that one device holds for one section and microbatch, no expert is named more than 1 times; in every section and microbatch one expert is named exactly 1 times by the blocks of every device.
All inputs are finite; a program needn't handle non-finite values.
Results may differ from a plain program's by a relative error of at most 0.024.
Values may be sent and summed in bfloat16 or wider, within the bound.
No kernel may reach another device: no remote copies, remote signals or barrier semaphores. Data moves between devices by JAX's collectives and lax.ppermute only.
A program may use at most 64 MiB of HBM per device.

v0:
```python
import functools

import jax
import jax.numpy as jnp
from jax import lax
from jax.experimental import pallas as pl
from jax.experimental.pallas import tpu as pltpu
from jax.sharding import PartitionSpec as P

H_CUT = 256
D_CUT = 512
K_CUT = 512
DOWN_PARTS = 3
SMALL = pltpu.CompilerParams(vmem_limit_bytes=8 * 1024 * 1024)


def in_vmem(x):
    return pltpu.with_memory_space_constraint(x, pltpu.VMEM)


def in_hbm(x):
    return pltpu.with_memory_space_constraint(x, pltpu.HBM)


def spec(space):
    return pl.BlockSpec(memory_space=space)


def normalised(hidden, gain_row):
    scaled = lax.rsqrt(jnp.mean(hidden * hidden, axis=-1, keepdims=True) + 1e-06)
    return (hidden * scaled * gain_row).astype(jnp.bfloat16)


def mixed(which, ids_ref, scores_ref, hidden_ref, returned_ref, block):
    topk = ids_ref.shape[1]
    parts = [scores_ref[which, k, block] for k in range(topk)]
    whole = parts[0]
    for k in range(1, topk):
        whole = whole + parts[k]
    total = None
    for k in range(topk):
        weight = jnp.full((1, 1), parts[k], jnp.float32) / jnp.full((1, 1), whole, jnp.float32)
        term = returned_ref[ids_ref[which, k, block]].astype(jnp.float32) * weight
        total = term if total is None else total + term
    return (hidden_ref[block].astype(jnp.float32) + total).astype(jnp.bfloat16)


def pack(ids, normed_ref, packed_ref):
    for expert in range(packed_ref.shape[0]):
        block = jnp.int32(0)
        for b in range(1, len(ids)):
            for one in ids[b]:
                block = jnp.where(one == expert, jnp.int32(b), block)
        packed_ref[expert] = normed_ref[block]


def table_ids(which, ids_ref):
    topk, blocks = ids_ref.shape[1:]
    return [[ids_ref[which, k, b] for k in range(topk)] for b in range(blocks)]


def first_kernel(
    core_ref, ro_h, rx_h, so_h, sx_h, x_hbm, go, gx, gate, up, down,
    hidden_ref, packed_ref, gains_ref, gate_v, up_v, down_v, ids_ref, scores_ref,
    ro, rx, so, sx, normed_ref, gain_v, sems, weight_sems,
):
    core = core_ref[0]
    first = core == 0
    pairs = (
        (ro_h, ro), (rx_h, rx), (so_h, so), (sx_h, sx),
        (go, gain_v.at[0]), (gx, gain_v.at[1]), (x_hbm.at[:, core], hidden_ref),
    )
    copies = [pltpu.make_async_copy(source, target, sems.at[i]) for i, (source, target) in enumerate(pairs)]
    for copy in copies:
        copy.start()
    for copy in copies:
        copy.wait()
    loads = [
        pltpu.make_async_copy(source, target, weight_sems.at[i])
        for i, (source, target) in enumerate(((gate, gate_v), (up, up_v), (down, down_v)))
    ]

    @pl.when(first)
    def _():
        for copy in loads:
            copy.start()

    topk, blocks = ro.shape
    ids = [[None] * topk for _ in range(blocks)]
    for b in range(blocks):
        for k in range(topk):
            ids[b][k] = jnp.where(first, ro[k, b], rx[k, b])
            ids_ref[0, k, b] = ids[b][k]
            ids_ref[1, k, b] = jnp.where(first, rx[k, b], ro[k, b])
            scores_ref[0, k, b] = jnp.where(first, so[k, b], sx[k, b])
            scores_ref[1, k, b] = jnp.where(first, sx[k, b], so[k, b])
    own = gain_v[0].astype(jnp.float32)
    other = gain_v[1].astype(jnp.float32)
    gain = jnp.where(first, own, other)
    gains_ref[0] = gain
    gains_ref[1] = jnp.where(first, other, own)
    for block in range(hidden_ref.shape[0]):
        normed_ref[block] = normalised(hidden_ref[block].astype(jnp.float32), gain)
    pack(ids, normed_ref, packed_ref)

    @pl.when(first)
    def _():
        for copy in loads:
            copy.wait()


def first_call(held, slots, core_table, route, route_x, score, score_x, whole_x, gain, gain_x, own):
    width = held[2]
    both = (2,) + route.shape
    return pl.pallas_call(
        first_kernel,
        out_shape=(
            pltpu.VMEM(held, jnp.bfloat16),
            pltpu.VMEM(slots, jnp.bfloat16),
            pltpu.VMEM((2, 1, width), jnp.float32),
            *[pltpu.VMEM(w.shape, w.dtype) for w in own],
            jax.ShapeDtypeStruct(both, jnp.int32),
            jax.ShapeDtypeStruct(both, jnp.float32),
        ),
        in_specs=[spec(pltpu.SMEM)] + [spec(pltpu.HBM)] * 10,
        out_specs=(spec(pltpu.VMEM),) * 6 + (spec(pltpu.SMEM),) * 2,
        scratch_shapes=[
            pltpu.SMEM(route.shape, jnp.int32),
            pltpu.SMEM(route.shape, jnp.int32),
            pltpu.SMEM(route.shape, jnp.float32),
            pltpu.SMEM(route.shape, jnp.float32),
            pltpu.VMEM(held, jnp.bfloat16),
            pltpu.VMEM((2, 1, width), jnp.bfloat16),
            pltpu.SemaphoreType.DMA((7,)),
            pltpu.SemaphoreType.DMA((3,)),
        ],
        compiler_params=SMALL,
        name="slice_norm_pack",
    )(core_table, *[in_hbm(v) for v in (route, route_x, score, score_x, whole_x, gain, gain_x, *own)])


def enter_kernel(ids_ref, hidden_ref, gains_ref, token_ref, packed_ref, normed_ref):
    del token_ref
    for block in range(hidden_ref.shape[0]):
        normed_ref[block] = normalised(hidden_ref[block].astype(jnp.float32), gains_ref[0])
    pack(table_ids(0, ids_ref), normed_ref, packed_ref)


def between_kernel(ids_ref, scores_ref, hidden_ref, returned_ref, gains_ref, out_ref, packed_ref, normed_ref):
    for block in range(hidden_ref.shape[0]):
        result = mixed(0, ids_ref, scores_ref, hidden_ref, returned_ref, block)
        out_ref[block] = result
        normed_ref[block] = normalised(result.astype(jnp.float32), gains_ref[1])
    pack(table_ids(1, ids_ref), normed_ref, packed_ref)


def leave_kernel(ids_ref, scores_ref, hidden_ref, returned_ref, out_ref, token_ref):
    token_ref[...] = jnp.zeros_like(token_ref)
    for block in range(hidden_ref.shape[0]):
        out_ref[block] = mixed(1, ids_ref, scores_ref, hidden_ref, returned_ref, block)


def small_call(kernel, name, outs, scratch, smem, vmem):
    single = len(outs) == 1
    shapes = tuple(pltpu.VMEM(o, jnp.bfloat16) for o in outs)
    specs = tuple(spec(pltpu.VMEM) for _ in outs)
    return pl.pallas_call(
        kernel,
        out_shape=shapes[0] if single else shapes,
        in_specs=[spec(pltpu.SMEM)] * len(smem) + [spec(pltpu.VMEM)] * len(vmem),
        out_specs=specs[0] if single else specs,
        scratch_shapes=[pltpu.VMEM(s, jnp.bfloat16) for s in scratch],
        compiler_params=SMALL,
        name=name,
    )(*smem, *[in_vmem(v) for v in vmem])


def silu_times(gate_part, up_part):
    return (gate_part / (1.0 + jnp.exp(-gate_part)) * up_part).astype(jnp.bfloat16)


def down_part(active_v, down_ref, out_ref):
    for c in range(down_ref.shape[1] // D_CUT):
        cut = pl.ds(c * D_CUT, D_CUT)
        produced = jnp.dot(active_v[...], down_ref[:, cut], preferred_element_type=jnp.float32)
        out_ref[:, cut] = produced.astype(jnp.bfloat16)


def load_copies(sources, targets, sems):
    (gate, up, down), (gate_ref, up_ref, down_ref) = sources, targets
    parts = gate_ref.shape[0] // K_CUT
    down_rows = down_ref.shape[0] // DOWN_PARTS
    made = []
    for c in range(parts):
        cut = pl.ds(c * K_CUT, K_CUT)
        made.append(pltpu.make_async_copy(gate.at[cut], gate_ref.at[cut], sems.at[2 * c]))
        made.append(pltpu.make_async_copy(up.at[cut], up_ref.at[cut], sems.at[2 * c + 1]))
    for c in range(DOWN_PARTS):
        cut = pl.ds(c * down_rows, down_rows)
        made.append(pltpu.make_async_copy(down.at[cut], down_ref.at[cut], sems.at[2 * parts + c]))
    return made


def streamed_ffn(x_ref, targets, out_ref, active_v, gate_sum, up_sum, waits):
    gate_ref, up_ref, down_ref = targets
    parts = gate_ref.shape[0] // K_CUT
    for c in range(parts):
        cut = pl.ds(c * K_CUT, K_CUT)
        for copy, weight_ref, sum_ref in ((waits[2 * c], gate_ref, gate_sum), (waits[2 * c + 1], up_ref, up_sum)):
            copy.wait()
            term = jnp.dot(x_ref[:, cut], weight_ref[cut, :], preferred_element_type=jnp.float32)
            sum_ref[...] = term if c == 0 else sum_ref[...] + term
    active_v[...] = silu_times(gate_sum[...], up_sum[...])
    for copy in waits[2 * parts :]:
        copy.wait()
    down_part(active_v, down_ref, out_ref)


def first_ffn_kernel(
    core_ref, x_ref, gi, ui, di, gb, ub, db, out_ref, gate_ref, up_ref, down_ref, active_v, gate_sum, up_sum, sems
):
    targets = (gate_ref, up_ref, down_ref)

    @pl.when(core_ref[0] == 0)
    def _():
        ffn_kernel(x_ref, *targets, out_ref, active_v)

    @pl.when(core_ref[0] != 0)
    def _():
        copies = load_copies((gb, ub, db), targets, sems)
        for copy in copies:
            copy.start()
        streamed_ffn(x_ref, targets, out_ref, active_v, gate_sum, up_sum, copies)


def second_ffn_kernel(
    core_ref, x_ref, ga, ua, da, gb, ub, db, out_ref, gate_ref, up_ref, down_ref, active_v, gate_sum, up_sum, sems
):
    targets = (gate_ref, up_ref, down_ref)

    @pl.when(core_ref[0] == 0)
    def _():
        for copy in load_copies((gb, ub, db), targets, sems):
            copy.start()

    @pl.when(core_ref[0] != 0)
    def _():
        for copy in load_copies((ga, ua, da), targets, sems):
            copy.start()

    waits = load_copies((ga, ua, da), targets, sems)
    streamed_ffn(x_ref, targets, out_ref, active_v, gate_sum, up_sum, waits)


def ffn_cost(flat, hidden):
    rows, width = flat.shape
    return pl.CostEstimate(
        flops=6 * rows * width * hidden,
        bytes_accessed=6 * width * hidden + 4 * rows * width,
        transcendentals=rows * hidden,
    )


def load_ffn(kernel, core_table, received, first, second, aliases):
    experts, rows, width = received.shape
    hidden = first[0].shape[1]
    flat = received.reshape(experts * rows, width)
    sums = pltpu.VMEM((flat.shape[0], hidden), jnp.float32)
    place, kind = (in_vmem, pltpu.VMEM) if aliases else (in_hbm, pltpu.HBM)
    produced, *weights = pl.pallas_call(
        kernel,
        out_shape=(pltpu.VMEM(flat.shape, jnp.bfloat16), *[pltpu.VMEM(w.shape, w.dtype) for w in first]),
        in_specs=[spec(pltpu.SMEM), spec(pltpu.VMEM)] + [spec(kind)] * 3 + [spec(pltpu.HBM)] * 3,
        out_specs=(spec(pltpu.VMEM),) * 4,
        scratch_shapes=[
            pltpu.VMEM((flat.shape[0], hidden), jnp.bfloat16),
            sums,
            sums,
            pltpu.SemaphoreType.DMA((2 * (width // K_CUT) + DOWN_PARTS,)),
        ],
        input_output_aliases=aliases,
        compiler_params=SMALL,
        cost_estimate=ffn_cost(flat, hidden),
        name="load_expert_ffn",
    )(core_table, in_vmem(flat), *[place(w) for w in first], *[in_hbm(w) for w in second])
    return produced.reshape(received.shape), weights


def ffn_kernel(x_ref, gate_ref, up_ref, down_ref, out_ref, active_v):
    for c in range(gate_ref.shape[1] // H_CUT):
        cut = pl.ds(c * H_CUT, H_CUT)
        gate_part = jnp.dot(x_ref[...], gate_ref[:, cut], preferred_element_type=jnp.float32)
        up_part = jnp.dot(x_ref[...], up_ref[:, cut], preferred_element_type=jnp.float32)
        active_v[:, cut] = silu_times(gate_part, up_part)
    down_part(active_v, down_ref, out_ref)


def ffn(received, weights):
    experts, rows, width = received.shape
    hidden = weights[0].shape[1]
    flat = received.reshape(experts * rows, width)
    produced = pl.pallas_call(
        ffn_kernel,
        out_shape=pltpu.VMEM(flat.shape, jnp.bfloat16),
        in_specs=[spec(pltpu.VMEM)] * 4,
        out_specs=spec(pltpu.VMEM),
        scratch_shapes=[pltpu.VMEM((flat.shape[0], hidden), jnp.bfloat16)],
        compiler_params=SMALL,
        cost_estimate=ffn_cost(flat, hidden),
        name="expert_ffn",
    )(in_vmem(flat), *[in_vmem(w) for w in weights])
    return produced.reshape(received.shape)


def exchange(slots):
    return lax.all_to_all(slots, "expert", 0, 0, tiled=True)


def shards(activations, norm_gain, w_gate, w_up, w_down, routes, gate_scores):
    sections = lax.axis_size("pipe")
    experts = lax.axis_size("expert")
    section = lax.axis_index("pipe")
    core = section % 2
    stage = section // 2
    stages = sections // 2
    blocks, topk = routes.shape[2:]
    rows = activations.shape[1] // blocks
    lane = rows // 2
    width = activations.shape[2]
    held = (blocks, lane, width)
    slots = (experts, lane, width)
    swap = [(i, i ^ 1) for i in range(sections)]

    def swapped(x):
        return lax.ppermute(x, "pipe", swap)

    route = routes[0, 0].T
    score = gate_scores[0, 0].T
    route_x, gain_x, score_x = swapped(route), swapped(norm_gain), swapped(score)
    own = (w_gate[0, 0], w_up[0, 0], w_down[0, 0])
    *own, route_x, gain_x, score_x = lax.optimization_barrier((*own, route_x, gain_x, score_x))
    other = tuple(swapped(w) for w in own)
    core_table = core.astype(jnp.int32).reshape(1)

    whole_x = activations[0].reshape(blocks, 2, lane, width)
    hidden, sent, gains, *weights_a, ids, scores = first_call(
        held, slots, core_table, route, route_x, score, score_x, whole_x, norm_gain, gain_x, own
    )
    out_a, out_b = [], []
    for step in range(stages):
        if step == 0:
            made, weights_a = load_ffn(
                first_ffn_kernel, core_table, exchange(sent), weights_a, other, {2: 1, 3: 2, 4: 3}
            )
        else:
            made = ffn(exchange(sent), weights_a)
        hidden, sent = small_call(
            between_kernel, "mix_norm_pack", (held, slots), (held,), (ids, scores), (hidden, exchange(made), gains)
        )
        out_a.append(hidden)
        if step == 0:
            made, weights_b = load_ffn(second_ffn_kernel, core_table, exchange(sent), own, other, {})
        else:
            made = ffn(exchange(sent), weights_b)
        hidden, token = small_call(
            leave_kernel, "mix", (held, (16, 128)), (), (ids, scores), (hidden, exchange(made))
        )
        out_b.append(hidden)
        if step < stages - 1:
            hidden = lax.ppermute(hidden, "pipe", [(i, i + 2) for i in range(sections - 2)])
            if step > 0:
                token = lax.ppermute(token, "pipe", [(i, i + 1) for i in range(0, sections, 2)])
            sent = small_call(enter_kernel, "norm_pack", (slots,), (held,), (ids,), (hidden, gains, token))

    def chosen(values):
        result = values[-1]
        for step in range(stages - 1):
            result = jnp.where(stage == step, values[step], result)
        return result

    result_a, result_b = chosen(out_a), chosen(out_b)
    kept = jnp.where(core == 0, result_a, result_b)
    got = swapped(jnp.where(core == 0, result_b, result_a))
    whole = jnp.where(core == 0, jnp.stack([kept, got], axis=1), jnp.stack([got, kept], axis=1))
    return whole.reshape(1, 1, blocks * rows, width)


def solution(mesh):
    in_specs = (
        P(None, "expert", None),
        P("pipe", None),
        P("pipe", "expert", None, None),
        P("pipe", "expert", None, None),
        P("pipe", "expert", None, None),
        P("pipe", None, "expert", None),
        P("pipe", None, "expert", None),
    )
    out_specs = P("pipe", None, "expert", None)
    return jax.shard_map(shards, mesh=mesh, in_specs=in_specs, out_specs=out_specs, check_vma=False)
```

profile of v0, /device:TPU:1, one launch (start us, length us, event | category | flops | bytes accessed | tf_op | source)
XLA Modules:
  0.0 346.6 jit_solution(15096250661322588852)
XLA Ops:
  0.0 1.4 collective-permute-start.1
  1.9 0.8 collective-permute-done.rx_h
  3.9 2.0 slice_norm_pack.1
  5.9 21.0 %all_to_all.80 = bf16[16,16,2048]{2,1,0:T(8,128)(2,1)S(1)} all-to-all(bf16[16,16,2048]{2,1,0:T(8,128)(2,1)S(1)} %get-tuple-element.51), channel_id=1, replica_groups=mesh['pipe'=8,'expert'=16] {'expert'}, dimensions={0} | all-to-all | bytes 2097152 | tf_op jit(solution)/shard_map/all_to_all | solution.py:316
  26.9 5.0 %load_expert_ffn.2 = (bf16[256,2048]{1,0:T(8,128)(2,1)S(1)}, bf16[2048,768]{1,0:T(8,128)(2,1)S(1)}, bf16[2048,768]{1,0:T(8,128)(2,1)S(1)}, bf16[768,2048]{1,0:T(8,128)(2,1)S(1)}) custom-call(s32[1]{0:T(128)} %bitcast.core_ref, bf16[256,2048]{1,0:T(8,128)(2,1)S(1)} %bitcast.31, ...), custom_call_target="tpu_custom_call", output_to_operand_aliasing={{1}: (2, {}), {2}: (3, {}), {3}: (4, {})} | custom-call | flops 2415919104 | bytes 11534336 | tf_op jit(solution)/shard_map/load_expert_ffn/pallas_call | solution.py:270
  31.9 17.8 %all_to_all.81.returned_ref = bf16[16,16,2048]{2,1,0:T(8,128)(2,1)S(1)} all-to-all(bf16[16,16,2048]{2,1,0:T(8,128)(2,1)S(1)} %bitcast.44), channel_id=1, replica_groups=mesh['pipe'=8,'expert'=16] {'expert'}, dimensions={0} | all-to-all | bytes 2097152 | tf_op jit(solution)/shard_map/all_to_all | solution.py:316
  49.7 1.0 mix_norm_pack.4
  50.7 16.1 %all_to_all.82 = bf16[16,16,2048]{2,1,0:T(8,128)(2,1)S(1)} all-to-all(bf16[16,16,2048]{2,1,0:T(8,128)(2,1)S(1)} %get-tuple-element.58), channel_id=1, replica_groups=mesh['pipe'=8,'expert'=16] {'expert'}, dimensions={0} | all-to-all | bytes 2097152 | tf_op jit(solution)/shard_map/all_to_all | solution.py:316
  66.8 5.0 %load_expert_ffn.3 = (bf16[256,2048]{1,0:T(8,128)(2,1)S(1)}, bf16[2048,768]{1,0:T(8,128)(2,1)S(1)}, bf16[2048,768]{1,0:T(8,128)(2,1)S(1)}, bf16[768,2048]{1,0:T(8,128)(2,1)S(1)}) custom-call(s32[1]{0:T(128)} %bitcast.core_ref, bf16[256,2048]{1,0:T(8,128)(2,1)S(1)} %bitcast.32, bf16[2048,768]{1,0:T(8,128)(2,1)} %bitcast.48, bf16[2048,768]{1,0:T(8,128)(2,1)} %bitcast.51, ...), custom_call_target="tpu_custom_call" | custom-call | flops 2415919104 | bytes 11534336 | tf_op jit(solution)/shard_map/load_expert_ffn/pallas_call | solution.py:270
  71.8 16.1 %all_to_all.83.returned_ref = bf16[16,16,2048]{2,1,0:T(8,128)(2,1)S(1)} all-to-all(bf16[16,16,2048]{2,1,0:T(8,128)(2,1)S(1)} %bitcast.45), channel_id=1, replica_groups=mesh['pipe'=8,'expert'=16] {'expert'}, dimensions={0} | all-to-all | bytes 2097152 | tf_op jit(solution)/shard_map/all_to_all | solution.py:316
  87.9 0.7 mix.4
  88.7 2.9 collective-permute-start.6
  91.6 3.3 collective-permute-done.6.hidden_ref
  94.9 0.8 norm_pack.3
  95.7 14.7 %all_to_all.84 = bf16[16,16,2048]{2,1,0:T(8,128)(2,1)S(1)} all-to-all(bf16[16,16,2048]{2,1,0:T(8,128)(2,1)S(1)} %norm_pack.3), channel_id=1, replica_groups=mesh['pipe'=8,'expert'=16] {'expert'}, dimensions={0} | all-to-all | bytes 2097152 | tf_op jit(solution)/shard_map/all_to_all | solution.py:316
  110.4 2.7 expert_ffn.6
  113.0 14.5 %all_to_all.85.returned_ref = bf16[16,16,2048]{2,1,0:T(8,128)(2,1)S(1)} all-to-all(bf16[16,16,2048]{2,1,0:T(8,128)(2,1)S(1)} %bitcast.38), channel_id=1, replica_groups=mesh['pipe'=8,'expert'=16] {'expert'}, dimensions={0} | all-to-all | bytes 2097152 | tf_op jit(solution)/shard_map/all_to_all | solution.py:316
  127.5 1.0 mix_norm_pack.5
  128.5 14.5 %all_to_all.86 = bf16[16,16,2048]{2,1,0:T(8,128)(2,1)S(1)} all-to-all(bf16[16,16,2048]{2,1,0:T(8,128)(2,1)S(1)} %get-tuple-element.66), channel_id=1, replica_groups=mesh['pipe'=8,'expert'=16] {'expert'}, dimensions={0} | all-to-all | bytes 2097152 | tf_op jit(solution)/shard_map/all_to_all | solution.py:316
  142.9 2.7 expert_ffn.7
  145.6 14.5 %all_to_all.87.returned_ref = bf16[16,16,2048]{2,1,0:T(8,128)(2,1)S(1)} all-to-all(bf16[16,16,2048]{2,1,0:T(8,128)(2,1)S(1)} %bitcast.39), channel_id=1, replica_groups=mesh['pipe'=8,'expert'=16] {'expert'}, dimensions={0} | all-to-all | bytes 2097152 | tf_op jit(solution)/shard_map/all_to_all | solution.py:316
  160.8 3.9 %collective-permute-start.7 = (bf16[4,16,2048]{2,1,0:T(8,128)(2,1)S(1)}, bf16[4,16,2048]{2,1,0:T(8,128)(2,1)S(1)}, u32[]{:S(2)}, u32[]{:S(2)}) collective-permute-start(bf16[4,16,2048]{2,1,0:T(8,128)(2,1)S(1)} %get-tuple-element.70), channel_id=1, source_target_pairs={{0,32},{16,48},{32,64},{48,80},{64,96},{80,112},{1,33},{17,49},{33... | collective-permute-start | bytes 786440 | tf_op jit(solution)/shard_map/ppermute | solution.py:370
  164.7 1.3 collective-permute-start.8
  166.0 12.6 %collective-permute-done.8.token_ref = bf16[16,128]{1,0:T(8,128)(2,1)S(1)} collective-permute-done((bf16[16,128]{1,0:T(8,128)(2,1)S(1)}, bf16[16,128]{1,0:T(8,128)(2,1)S(1)}, u32[]{:S(2)}, u32[]{:S(2)}) %collective-permute-start.8) | collective-permute-done | bytes 4128 | tf_op jit(solution)/shard_map/ppermute | solution.py:372
  178.7 0.8 norm_pack.4
  179.5 18.2 %all_to_all.88 = bf16[16,16,2048]{2,1,0:T(8,128)(2,1)S(1)} all-to-all(bf16[16,16,2048]{2,1,0:T(8,128)(2,1)S(1)} %norm_pack.4), channel_id=1, replica_groups=mesh['pipe'=8,'expert'=16] {'expert'}, dimensions={0} | all-to-all | bytes 2097152 | tf_op jit(solution)/shard_map/all_to_all | solution.py:316
  197.7 2.7 expert_ffn.8
  200.3 16.6 %all_to_all.89.returned_ref = bf16[16,16,2048]{2,1,0:T(8,128)(2,1)S(1)} all-to-all(bf16[16,16,2048]{2,1,0:T(8,128)(2,1)S(1)} %bitcast.41), channel_id=1, replica_groups=mesh['pipe'=8,'expert'=16] {'expert'}, dimensions={0} | all-to-all | bytes 2097152 | tf_op jit(solution)/shard_map/all_to_all | solution.py:316
  216.9 1.0 mix_norm_pack.6
  217.9 15.9 %all_to_all.90 = bf16[16,16,2048]{2,1,0:T(8,128)(2,1)S(1)} all-to-all(bf16[16,16,2048]{2,1,0:T(8,128)(2,1)S(1)} %get-tuple-element.73), channel_id=1, replica_groups=mesh['pipe'=8,'expert'=16] {'expert'}, dimensions={0} | all-to-all | bytes 2097152 | tf_op jit(solution)/shard_map/all_to_all | solution.py:316
  233.8 2.7 expert_ffn.9
  236.4 15.3 %all_to_all.91.returned_ref = bf16[16,16,2048]{2,1,0:T(8,128)(2,1)S(1)} all-to-all(bf16[16,16,2048]{2,1,0:T(8,128)(2,1)S(1)} %bitcast.43), channel_id=1, replica_groups=mesh['pipe'=8,'expert'=16] {'expert'}, dimensions={0} | all-to-all | bytes 2097152 | tf_op jit(solution)/shard_map/all_to_all | solution.py:316
  252.4 1.3 collective-permute-start.9
  253.8 1.3 collective-permute-start.10
  255.1 6.7 %collective-permute-done.10.token_ref = bf16[16,128]{1,0:T(8,128)(2,1)S(1)} collective-permute-done((bf16[16,128]{1,0:T(8,128)(2,1)S(1)}, bf16[16,128]{1,0:T(8,128)(2,1)S(1)}, u32[]{:S(2)}, u32[]{:S(2)}) %collective-permute-start.10) | collective-permute-done | bytes 4128 | tf_op jit(solution)/shard_map/ppermute | solution.py:372
  261.7 0.8 norm_pack.5
  262.5 18.2 %all_to_all.92 = bf16[16,16,2048]{2,1,0:T(8,128)(2,1)S(1)} all-to-all(bf16[16,16,2048]{2,1,0:T(8,128)(2,1)S(1)} %norm_pack.5), channel_id=1, replica_groups=mesh['pipe'=8,'expert'=16] {'expert'}, dimensions={0} | all-to-all | bytes 2097152 | tf_op jit(solution)/shard_map/all_to_all | solution.py:316
  280.7 2.7 expert_ffn.10
  283.4 16.6 %all_to_all.93.returned_ref = bf16[16,16,2048]{2,1,0:T(8,128)(2,1)S(1)} all-to-all(bf16[16,16,2048]{2,1,0:T(8,128)(2,1)S(1)} %bitcast.34), channel_id=1, replica_groups=mesh['pipe'=8,'expert'=16] {'expert'}, dimensions={0} | all-to-all | bytes 2097152 | tf_op jit(solution)/shard_map/all_to_all | solution.py:316
  300.0 1.0 mix_norm_pack.7
  300.9 15.9 %all_to_all.94 = bf16[16,16,2048]{2,1,0:T(8,128)(2,1)S(1)} all-to-all(bf16[16,16,2048]{2,1,0:T(8,128)(2,1)S(1)} %get-tuple-element.77), channel_id=1, replica_groups=mesh['pipe'=8,'expert'=16] {'expert'}, dimensions={0} | all-to-all | bytes 2097152 | tf_op jit(solution)/shard_map/all_to_all | solution.py:316
  316.8 3.7 %expert_ffn.11 = bf16[256,2048]{1,0:T(8,128)(2,1)} custom-call(bf16[256,2048]{1,0:T(8,128)(2,1)S(1)} %bitcast.35, bf16[2048,768]{1,0:T(8,128)(2,1)S(1)} %get-tuple-element.67.gate_ref, bf16[2048,768]{1,0:T(8,128)(2,1)S(1)} %get-tuple-element.68.up_ref, bf16[768,2048]{1,0:T(8,128)(2,1)S(1)} %get-tuple-element.69.down_ref), custom_call_target="tpu_custom_call" | custom-call | flops 2415919104 | bytes 11534336 | tf_op jit(solution)/shard_map/expert_ffn/pallas_call | solution.py:302
  320.5 3.7 %all-to-all-start.15 = ((bf16[16,16,2048]{2,1,0:T(8,128)(2,1)}), bf16[16,16,2048]{2,1,0:T(8,128)(2,1)S(1)}, u32[]{:S(2)}, u32[]{:S(2)}) async-start(bf16[16,16,2048]{2,1,0:T(8,128)(2,1)} %bitcast.25), calls=%async_computation.15 | async-start | bytes 2097152 | tf_op jit(solution)/shard_map/all_to_all | solution.py:316
  324.2 12.9 %all-to-all-done.15.returned_ref = bf16[16,16,2048]{2,1,0:T(8,128)(2,1)S(1)} async-done(((bf16[16,16,2048]{2,1,0:T(8,128)(2,1)}), bf16[16,16,2048]{2,1,0:T(8,128)(2,1)S(1)}, u32[]{:S(2)}, u32[]{:S(2)}) %all-to-all-start.15) | async-done | bytes 1048608 | tf_op jit(solution)/shard_map/all_to_all | solution.py:316
  337.0 1.3 mix.7
  338.4 6.1 %collective-permute-start.11 = (bf16[4,16,2048]{2,1,0:T(8,128)(2,1)S(1)}, bf16[4,16,2048]{2,1,0:T(8,128)(2,1)S(1)}, u32[]{:S(2)}, u32[]{:S(2)}) collective-permute-start(bf16[4,16,2048]{2,1,0:T(8,128)(2,1)S(1)} %broadcast_select_fusion), channel_id=1, source_target_pairs={{0,16},{16,0},{32,48},{48,32},{64,80},{80,64},{96,112},{112,96},{1... | collective-permute-start | bytes 786440 | tf_op jit(solution)/shard_map/ppermute | solution.py:335
  344.5 1.2 collective-permute-done.11
  345.8 0.8 copy.11
  (23 shorter events, 3.3 us)
Async XLA Ops:
  0.0 3.0 collective-permute-start.1
  1.4 1.4 collective-permute-start
  1.4 1.5 collective-permute-start.2
  2.8 1.1 copy-start.1
  3.0 0.9 copy-start.2
  3.0 0.9 copy-start
  3.0 23.9 %collective-permute-start.3 = (bf16[2048,768]{1,0:T(8,128)(2,1)}, bf16[2048,768]{1,0:T(8,128)(2,1)}, u32[]{:S(2)}, u32[]{:S(2)}) collective-permute-start(bf16[2048,768]{1,0:T(8,128)(2,1)} %bitcast.46), channel_id=1, source_target_pairs={{0,16},{16,0},{32,48},{48,32},{64,80},{80,64},{96,112},{112,96},{1... | collective-permute-start | bytes 9437192 | tf_op jit(solution)/shard_map/ppermute | solution.py:335
  3.4 23.5 %collective-permute-start.4 = (bf16[2048,768]{1,0:T(8,128)(2,1)}, bf16[2048,768]{1,0:T(8,128)(2,1)}, u32[]{:S(2)}, u32[]{:S(2)}) collective-permute-start(bf16[2048,768]{1,0:T(8,128)(2,1)} %bitcast.49), channel_id=1, source_target_pairs={{0,16},{16,0},{32,48},{48,32},{64,80},{80,64},{96,112},{112,96},{1... | collective-permute-start | bytes 9437192 | tf_op jit(solution)/shard_map/ppermute | solution.py:335
  3.5 23.4 %collective-permute-start.5 = (bf16[768,2048]{1,0:T(8,128)(2,1)}, bf16[768,2048]{1,0:T(8,128)(2,1)}, u32[]{:S(2)}, u32[]{:S(2)}) collective-permute-start(bf16[768,2048]{1,0:T(8,128)(2,1)} %bitcast.52), channel_id=1, source_target_pairs={{0,16},{16,0},{32,48},{48,32},{64,80},{80,64},{96,112},{112,96},{1... | collective-permute-start | bytes 9437192 | tf_op jit(solution)/shard_map/ppermute | solution.py:335
  88.7 6.2 %collective-permute-start.6 = (bf16[4,16,2048]{2,1,0:T(8,128)(2,1)S(1)}, bf16[4,16,2048]{2,1,0:T(8,128)(2,1)S(1)}, u32[]{:S(2)}, u32[]{:S(2)}) collective-permute-start(bf16[4,16,2048]{2,1,0:T(8,128)(2,1)S(1)} %get-tuple-element.60), channel_id=1, source_target_pairs={{0,32},{16,48},{32,64},{48,80},{64,96},{80,112},{1,33},{17,49},{33... | collective-permute-start | bytes 786440 | tf_op jit(solution)/shard_map/ppermute | solution.py:370
  160.8 17.9 %collective-permute-start.7 = (bf16[4,16,2048]{2,1,0:T(8,128)(2,1)S(1)}, bf16[4,16,2048]{2,1,0:T(8,128)(2,1)S(1)}, u32[]{:S(2)}, u32[]{:S(2)}) collective-permute-start(bf16[4,16,2048]{2,1,0:T(8,128)(2,1)S(1)} %get-tuple-element.70), channel_id=1, source_target_pairs={{0,32},{16,48},{32,64},{48,80},{64,96},{80,112},{1,33},{17,49},{33... | collective-permute-start | bytes 786440 | tf_op jit(solution)/shard_map/ppermute | solution.py:370
  164.7 13.9 %collective-permute-start.8 = (bf16[16,128]{1,0:T(8,128)(2,1)S(1)}, bf16[16,128]{1,0:T(8,128)(2,1)S(1)}, u32[]{:S(2)}, u32[]{:S(2)}) collective-permute-start(bf16[16,128]{1,0:T(8,128)(2,1)S(1)} %get-tuple-element.71), channel_id=1, source_target_pairs={{0,16},{32,48},{64,80},{96,112},{1,17},{33,49},{65,81},{97,113},{2... | collective-permute-start | bytes 12296 | tf_op jit(solution)/shard_map/ppermute | solution.py:372
  252.4 9.3 %collective-permute-start.9 = (bf16[4,16,2048]{2,1,0:T(8,128)(2,1)S(1)}, bf16[4,16,2048]{2,1,0:T(8,128)(2,1)S(1)}, u32[]{:S(2)}, u32[]{:S(2)}) collective-permute-start(bf16[4,16,2048]{2,1,0:T(8,128)(2,1)S(1)} %get-tuple-element.74), channel_id=1, source_target_pairs={{0,32},{16,48},{32,64},{48,80},{64,96},{80,112},{1,33},{17,49},{33... | collective-permute-start | bytes 786440 | tf_op jit(solution)/shard_map/ppermute | solution.py:370
  253.8 8.0 %collective-permute-start.10 = (bf16[16,128]{1,0:T(8,128)(2,1)S(1)}, bf16[16,128]{1,0:T(8,128)(2,1)S(1)}, u32[]{:S(2)}, u32[]{:S(2)}) collective-permute-start(bf16[16,128]{1,0:T(8,128)(2,1)S(1)} %get-tuple-element.75), channel_id=1, source_target_pairs={{0,16},{32,48},{64,80},{96,112},{1,17},{33,49},{65,81},{97,113},{2... | collective-permute-start | bytes 12296 | tf_op jit(solution)/shard_map/ppermute | solution.py:372
  320.5 16.5 %all-to-all-start.15 = ((bf16[16,16,2048]{2,1,0:T(8,128)(2,1)}), bf16[16,16,2048]{2,1,0:T(8,128)(2,1)S(1)}, u32[]{:S(2)}, u32[]{:S(2)}) async-start(bf16[16,16,2048]{2,1,0:T(8,128)(2,1)} %bitcast.25), calls=%async_computation.15 | async-start | bytes 2097152 | tf_op jit(solution)/shard_map/all_to_all | solution.py:316
  338.4 7.3 %collective-permute-start.11 = (bf16[4,16,2048]{2,1,0:T(8,128)(2,1)S(1)}, bf16[4,16,2048]{2,1,0:T(8,128)(2,1)S(1)}, u32[]{:S(2)}, u32[]{:S(2)}) collective-permute-start(bf16[4,16,2048]{2,1,0:T(8,128)(2,1)S(1)} %broadcast_select_fusion), channel_id=1, source_target_pairs={{0,16},{16,0},{32,48},{48,32},{64,80},{80,64},{96,112},{112,96},{1... | collective-permute-start | bytes 786440 | tf_op jit(solution)/shard_map/ppermute | solution.py:335
where the time goes:
time: 347 us
  blocking collectives  246 us (71%)
  Pallas kernels  38.5 us (11%)
  waiting for transfers between devices  37.7 us (11%)
  starting transfers between devices  23.3 us (7%)
    all_to_all x15, blocking collectives, exchange(): return lax.all_to_all(slots, 'expert', 0, 0, tiled=True)  246 us
    ppermute x2, waiting for transfers between devices, shards(): lax.ppermute(token, 'pipe', [(i, i + 1) for i in range(0, sections, 2)])  19.3 us
    pallas_call x6, Pallas kernels, ffn(): pl.pallas_call(ffn_kernel, out_shape=pltpu.VMEM(flat.shape, jnp.bfloat16)...  17 us
    all_to_all x1, waiting for transfers between devices, exchange(): return lax.all_to_all(slots, 'expert', 0, 0, tiled=True)  12.9 us
    pallas_call x2, Pallas kernels, load_ffn(): pl.pallas_call(kernel, out_shape=(pltpu.VMEM(flat.shape, jnp.bfloat16), *...  9.94 us
    pallas_call x11, Pallas kernels, small_call(): pl.pallas_call(kernel, out_shape=shapes[0] if single else shapes, in_spec...  9.67 us
    ppermute x7, starting transfers between devices, swapped(): return lax.ppermute(x, 'pipe', swap)  8.94 us
    ppermute x3, starting transfers between devices, shards(): lax.ppermute(hidden, 'pipe', [(i, i + 2) for i in range(sections - 2)])  8.15 us
  transfers between devices with their start and end apart: 13, of which 7 were waited for; matrix products, arithmetic and copies ran while one was open for 0% of the time, Pallas kernels for 1%

commit v1 on v0

--- a/solution.py
+++ b/solution.py
@@ -9,6 +9,7 @@
 
 H_CUT = 256
 D_CUT = 512
+HELD = (1,)
 K_CUT = 512
 DOWN_PARTS = 3
 SMALL = pltpu.CompilerParams(vmem_limit_bytes=8 * 1024 * 1024)
@@ -24,6 +25,10 @@
 
 def spec(space):
     return pl.BlockSpec(memory_space=space)
+
+
+def core_of(section_ref):
+    return section_ref[0] & 1
 
 
 def normalised(hidden, gain_row):
@@ -60,11 +65,11 @@
 
 
 def first_kernel(
-    core_ref, ro_h, rx_h, so_h, sx_h, x_hbm, go, gx, gate, up, down,
+    section_ref, rx_h, sx_h, gx, ro_h, so_h, go, x_hbm, gate, up, down,
     hidden_ref, packed_ref, gains_ref, gate_v, up_v, down_v, ids_ref, scores_ref,
     ro, rx, so, sx, normed_ref, gain_v, sems, weight_sems,
 ):
-    core = core_ref[0]
+    core = core_of(section_ref)
     first = core == 0
     pairs = (
         (ro_h, ro), (rx_h, rx), (so_h, so), (sx_h, sx),
@@ -79,11 +84,6 @@
         pltpu.make_async_copy(source, target, weight_sems.at[i])
         for i, (source, target) in enumerate(((gate, gate_v), (up, up_v), (down, down_v)))
     ]
-
-    @pl.when(first)
-    def _():
-        for copy in loads:
-            copy.start()
 
     topk, blocks = ro.shape
     ids = [[None] * topk for _ in range(blocks)]
@@ -106,10 +106,12 @@
     @pl.when(first)
     def _():
         for copy in loads:
+            copy.start()
+        for copy in loads:
             copy.wait()
 
 
-def first_call(held, slots, core_table, route, route_x, score, score_x, whole_x, gain, gain_x, own):
+def first_call(held, slots, section_table, route, route_x, score, score_x, whole_x, gain, gain_x, own):
     width = held[2]
     both = (2,) + route.shape
     return pl.pallas_call(
@@ -122,7 +124,7 @@
             jax.ShapeDtypeStruct(both, jnp.int32),
             jax.ShapeDtypeStruct(both, jnp.float32),
         ),
-        in_specs=[spec(pltpu.SMEM)] + [spec(pltpu.HBM)] * 10,
+        in_specs=[spec(pltpu.SMEM)] + [spec(pl.ANY)] * 3 + [spec(pltpu.HBM)] * 7,
         out_specs=(spec(pltpu.VMEM),) * 6 + (spec(pltpu.SMEM),) * 2,
         scratch_shapes=[
             pltpu.SMEM(route.shape, jnp.int32),
@@ -136,11 +138,11 @@
         ],
         compiler_params=SMALL,
         name="slice_norm_pack",
-    )(core_table, *[in_hbm(v) for v in (route, route_x, score, score_x, whole_x, gain, gain_x, *own)])
-
-
-def enter_kernel(ids_ref, hidden_ref, gains_ref, token_ref, packed_ref, normed_ref):
-    del token_ref
+    )(section_table, route_x, score_x, gain_x, *[in_hbm(v) for v in (route, score, gain, whole_x, *own)])
+
+
+def enter_kernel(ids_ref, hidden_ref, gains_ref, *refs):
+    packed_ref, normed_ref = refs[-2:]
     for block in range(hidden_ref.shape[0]):
         normed_ref[block] = normalised(hidden_ref[block].astype(jnp.float32), gains_ref[0])
     pack(table_ids(0, ids_ref), normed_ref, packed_ref)
@@ -158,6 +160,61 @@
     token_ref[...] = jnp.zeros_like(token_ref)
     for block in range(hidden_ref.shape[0]):
         out_ref[block] = mixed(1, ids_ref, scores_ref, hidden_ref, returned_ref, block)
+
+
+def finish_kernel(section_ref, ids_ref, scores_ref, hidden_ref, returned_ref, *refs):
+    earlier, (kept_ref, sent_ref, last_ref, sems) = refs[:-4], refs[-4:]
+    stages = (len(earlier) + 1) // 2
+    for block in range(hidden_ref.shape[0]):
+        last_ref[block] = mixed(1, ids_ref, scores_ref, hidden_ref, returned_ref, block)
+    results_a, results_b = earlier[:stages], (*earlier[stages:], last_ref)
+    for step in range(stages):
+        for core, targets in ((0, (kept_ref, sent_ref)), (1, (sent_ref, kept_ref))):
+
+            @pl.when(section_ref[0] == 2 * step + core)
+            def _():
+                for i, source in enumerate((results_a[step], results_b[step])):
+                    pltpu.make_async_copy(source, targets[i], sems.at[i]).start()
+
+    for i, target in enumerate((kept_ref, sent_ref)):
+        pltpu.make_async_copy(results_a[0], target, sems.at[i]).wait()
+
+
+def finish(section_table, ids, scores, hidden, returned, earlier):
+    held = hidden.shape
+    return pl.pallas_call(
+        finish_kernel,
+        out_shape=(pltpu.VMEM(held, jnp.bfloat16),) * 2,
+        in_specs=[spec(pltpu.SMEM)] * 3 + [spec(pltpu.VMEM)] * 2 + [spec(pl.ANY)] * len(earlier),
+        out_specs=(spec(pltpu.VMEM),) * 2,
+        scratch_shapes=[pltpu.VMEM(held, jnp.bfloat16), pltpu.SemaphoreType.DMA((2,))],
+        compiler_params=SMALL,
+        name="mix_choose",
+    )(section_table, ids, scores, in_vmem(hidden), in_vmem(returned), *earlier)
+
+
+def join_kernel(section_ref, kept_ref, got_ref, out_ref, sems):
+    copies = [
+        pltpu.make_async_copy(kept_ref, out_ref.at[:, core_of(section_ref)], sems.at[0]),
+        pltpu.make_async_copy(got_ref, out_ref.at[:, 1 - core_of(section_ref)], sems.at[1]),
+    ]
+    for copy in copies:
+        copy.start()
+    for copy in copies:
+        copy.wait()
+
+
+def join(section_table, kept, got):
+    blocks, lane, width = kept.shape
+    return pl.pallas_call(
+        join_kernel,
+        out_shape=pltpu.HBM((blocks, 2, lane, width), jnp.bfloat16),
+        in_specs=[spec(pltpu.SMEM)] + [spec(pltpu.VMEM)] * 2,
+        out_specs=spec(pltpu.HBM),
+        scratch_shapes=[pltpu.SemaphoreType.DMA((2,))],
+        compiler_params=SMALL,
+        name="join_rows",
+    )(section_table, in_vmem(kept), in_vmem(got))
 
 
 def small_call(kernel, name, outs, scratch, smem, vmem):
@@ -201,7 +258,7 @@
     return made
 
 
-def streamed_ffn(x_ref, targets, out_ref, active_v, gate_sum, up_sum, waits):
+def streamed_ffn(x_ref, targets, out_ref, active_v, gate_sum, up_sum, down_sum, waits):
     gate_ref, up_ref, down_ref = targets
     parts = gate_ref.shape[0] // K_CUT
     for c in range(parts):
@@ -211,45 +268,53 @@
             term = jnp.dot(x_ref[:, cut], weight_ref[cut, :], preferred_element_type=jnp.float32)
             sum_ref[...] = term if c == 0 else sum_ref[...] + term
     active_v[...] = silu_times(gate_sum[...], up_sum[...])
-    for copy in waits[2 * parts :]:
-        copy.wait()
-    down_part(active_v, down_ref, out_ref)
+    down_rows = down_ref.shape[0] // DOWN_PARTS
+    for c in range(DOWN_PARTS):
+        waits[2 * parts + c].wait()
+        cut = pl.ds(c * down_rows, down_rows)
+        term = jnp.dot(active_v[:, cut], down_ref[cut, :], preferred_element_type=jnp.float32)
+        if c == 0:
+            down_sum[...] = term
+        elif c < DOWN_PARTS - 1:
+            down_sum[...] += term
+        else:
+            out_ref[...] = (down_sum[...] + term).astype(jnp.bfloat16)
 
 
 def first_ffn_kernel(
-    core_ref, x_ref, gi, ui, di, gb, ub, db, out_ref, gate_ref, up_ref, down_ref, active_v, gate_sum, up_sum, sems
+    section_ref, x_ref, gi, ui, di, gb, ub, db, out_ref, gate_ref, up_ref, down_ref, active_v, gate_sum, up_sum, down_sum, sems
 ):
     targets = (gate_ref, up_ref, down_ref)
 
-    @pl.when(core_ref[0] == 0)
+    @pl.when(core_of(section_ref) == 0)
     def _():
         ffn_kernel(x_ref, *targets, out_ref, active_v)
 
-    @pl.when(core_ref[0] != 0)
+    @pl.when(core_of(section_ref) != 0)
     def _():
         copies = load_copies((gb, ub, db), targets, sems)
         for copy in copies:
             copy.start()
-        streamed_ffn(x_ref, targets, out_ref, active_v, gate_sum, up_sum, copies)
+        streamed_ffn(x_ref, targets, out_ref, active_v, gate_sum, up_sum, down_sum, copies)
 
 
 def second_ffn_kernel(
-    core_ref, x_ref, ga, ua, da, gb, ub, db, out_ref, gate_ref, up_ref, down_ref, active_v, gate_sum, up_sum, sems
+    section_ref, x_ref, ga, ua, da, gb, ub, db, out_ref, gate_ref, up_ref, down_ref, active_v, gate_sum, up_sum, down_sum, sems
 ):
     targets = (gate_ref, up_ref, down_ref)
 
-    @pl.when(core_ref[0] == 0)
+    @pl.when(core_of(section_ref) == 0)
     def _():
         for copy in load_copies((gb, ub, db), targets, sems):
             copy.start()
 
-    @pl.when(core_ref[0] != 0)
+    @pl.when(core_of(section_ref) != 0)
     def _():
         for copy in load_copies((ga, ua, da), targets, sems):
             copy.start()
 
     waits = load_copies((ga, ua, da), targets, sems)
-    streamed_ffn(x_ref, targets, out_ref, active_v, gate_sum, up_sum, waits)
+    streamed_ffn(x_ref, targets, out_ref, active_v, gate_sum, up_sum, down_sum, waits)
 
 
 def ffn_cost(flat, hidden):
@@ -261,7 +326,7 @@
     )
 
 
-def load_ffn(kernel, core_table, received, first, second, aliases):
+def load_ffn(kernel, section_table, received, first, second, aliases):
     experts, rows, width = received.shape
     hidden = first[0].shape[1]
     flat = received.reshape(experts * rows, width)
@@ -270,19 +335,20 @@
     produced, *weights = pl.pallas_call(
         kernel,
         out_shape=(pltpu.VMEM(flat.shape, jnp.bfloat16), *[pltpu.VMEM(w.shape, w.dtype) for w in first]),
-        in_specs=[spec(pltpu.SMEM), spec(pltpu.VMEM)] + [spec(kind)] * 3 + [spec(pltpu.HBM)] * 3,
+        in_specs=[spec(pltpu.SMEM), spec(pltpu.VMEM)] + [spec(kind)] * 3 + [spec(pl.ANY)] * 3,
         out_specs=(spec(pltpu.VMEM),) * 4,
         scratch_shapes=[
             pltpu.VMEM((flat.shape[0], hidden), jnp.bfloat16),
             sums,
             sums,
+            pltpu.VMEM(flat.shape, jnp.float32),
             pltpu.SemaphoreType.DMA((2 * (width // K_CUT) + DOWN_PARTS,)),
         ],
         input_output_aliases=aliases,
         compiler_params=SMALL,
         cost_estimate=ffn_cost(flat, hidden),
         name="load_expert_ffn",
-    )(core_table, in_vmem(flat), *[place(w) for w in first], *[in_hbm(w) for w in second])
+    )(section_table, in_vmem(flat), *[place(w) for w in first], *second)
     return produced.reshape(received.shape), weights
 
 
@@ -320,8 +386,6 @@
     sections = lax.axis_size("pipe")
     experts = lax.axis_size("expert")
     section = lax.axis_index("pipe")
-    core = section % 2
-    stage = section // 2
     stages = sections // 2
     blocks, topk = routes.shape[2:]
     rows = activations.shape[1] // blocks
@@ -340,17 +404,17 @@
     own = (w_gate[0, 0], w_up[0, 0], w_down[0, 0])
     *own, route_x, gain_x, score_x = lax.optimization_barrier((*own, route_x, gain_x, score_x))
     other = tuple(swapped(w) for w in own)
-    core_table = core.astype(jnp.int32).reshape(1)
+    section_table = section.astype(jnp.int32).reshape(1)
 
     whole_x = activations[0].reshape(blocks, 2, lane, width)
     hidden, sent, gains, *weights_a, ids, scores = first_call(
-        held, slots, core_table, route, route_x, score, score_x, whole_x, norm_gain, gain_x, own
+        held, slots, section_table, route, route_x, score, score_x, whole_x, norm_gain, gain_x, own
     )
     out_a, out_b = [], []
     for step in range(stages):
         if step == 0:
             made, weights_a = load_ffn(
-                first_ffn_kernel, core_table, exchange(sent), weights_a, other, {2: 1, 3: 2, 4: 3}
+                first_ffn_kernel, section_table, exchange(sent), weights_a, other, {2: 1, 3: 2, 4: 3}
             )
         else:
             made = ffn(exchange(sent), weights_a)
@@ -359,29 +423,22 @@
         )
         out_a.append(hidden)
         if step == 0:
-            made, weights_b = load_ffn(second_ffn_kernel, core_table, exchange(sent), own, other, {})
+            made, weights_b = load_ffn(second_ffn_kernel, section_table, exchange(sent), own, other, {})
         else:
             made = ffn(exchange(sent), weights_b)
-        hidden, token = small_call(
-            leave_kernel, "mix", (held, (16, 128)), (), (ids, scores), (hidden, exchange(made))
-        )
+        back = exchange(made)
+        if step == stages - 1:
+            break
+        hidden, token = small_call(leave_kernel, "mix", (held, (16, 128)), (), (ids, scores), (hidden, back))
         out_b.append(hidden)
-        if step < stages - 1:
-            hidden = lax.ppermute(hidden, "pipe", [(i, i + 2) for i in range(sections - 2)])
-            if step > 0:
-                token = lax.ppermute(token, "pipe", [(i, i + 1) for i in range(0, sections, 2)])
-            sent = small_call(enter_kernel, "norm_pack", (slots,), (held,), (ids,), (hidden, gains, token))
-
-    def chosen(values):
-        result = values[-1]
-        for step in range(stages - 1):
-            result = jnp.where(stage == step, values[step], result)
-        return result
-
-    result_a, result_b = chosen(out_a), chosen(out_b)
-    kept = jnp.where(core == 0, result_a, result_b)
-    got = swapped(jnp.where(core == 0, result_b, result_a))
-    whole = jnp.where(core == 0, jnp.stack([kept, got], axis=1), jnp.stack([got, kept], axis=1))
+        hidden = lax.ppermute(hidden, "pipe", [(i, (i + 2) % sections) for i in range(sections)])
+        tokens = ()
+        if step in HELD:
+            tokens = (lax.ppermute(token, "pipe", [(i, i + 1) for i in range(0, sections, 2)]),)
+        sent = small_call(enter_kernel, "norm_pack", (slots,), (held,), (ids,), (hidden, gains, *tokens))
+
+    kept, leaving = finish(section_table, ids, scores, hidden, back, out_a + out_b)
+    whole = join(section_table, kept, swapped(leaving))
     return whole.reshape(1, 1, blocks * rows, width)
 
 

time: 347 us -> 335 us (0.965)
  waiting for transfers between devices: 37.7 us -> 26.1 us
    all_to_all x1 -> x0, waiting for transfers between devices: 12.9 us -> none  [exchange(): return lax.all_to_all(slots, 'expert', 0, 0, tiled=True)]
    ppermute x3, waiting for transfers between devices: 3.29 us -> 11.1 us  [shards(): lax.ppermute(hidden, 'pipe', [(i, (i + 2) % sections) for i in range(sect...]
    ppermute x7, starting transfers between devices: 8.94 us -> 16.7 us  [swapped(): return lax.ppermute(x, 'pipe', swap)]
    ppermute x2 -> x1, waiting for transfers between devices: 19.3 us -> 12.9 us  [shards(): lax.ppermute(token, 'pipe', [(i, i + 1) for i in range(0, sections, 2)])]
    all_to_all x1 -> x0, starting transfers between devices: 3.65 us -> none  [exchange(): return lax.all_to_all(slots, 'expert', 0, 0, tiled=True)]
    all_to_all x15 -> x16, blocking collectives: 246 us -> 244 us  [exchange(): return lax.all_to_all(slots, 'expert', 0, 0, tiled=True)]
    pallas_call x11 -> x10, Pallas kernels: 9.67 us -> 9.47 us  [small_call(): pl.pallas_call(kernel, out_shape=shapes[0] if single else shapes, in_spec...]
  transfers between devices with their start and end apart: 13 -> 11, of which waited for: 7 -> 6; matrix products, arithmetic and copies ran while one was open for 0% -> 0% of each run, Pallas kernels for 1% -> 1%
where the time goes in v1:
time: 335 us; the launch traced here: 334 us
  blocking collectives  244 us (73%)
  Pallas kernels  38.8 us (12%)
  waiting for transfers between devices  26.1 us (8%)
  starting transfers between devices  24.4 us (7%)
    all_to_all x16, blocking collectives, exchange(): return lax.all_to_all(slots, 'expert', 0, 0, tiled=True)  244 us
    ppermute x7, starting transfers between devices, swapped(): return lax.ppermute(x, 'pipe', swap)  16.7 us
    pallas_call x6, Pallas kernels, ffn(): pl.pallas_call(ffn_kernel, out_shape=pltpu.VMEM(flat.shape, jnp.bfloat16)...  15.8 us
    ppermute x1, waiting for transfers between devices, shards(): lax.ppermute(token, 'pipe', [(i, i + 1) for i in range(0, sections, 2)])  12.9 us
    ppermute x3, waiting for transfers between devices, shards(): lax.ppermute(hidden, 'pipe', [(i, (i + 2) % sections) for i in range(sect...  11.1 us
    pallas_call x2, Pallas kernels, load_ffn(): pl.pallas_call(kernel, out_shape=(pltpu.VMEM(flat.shape, jnp.bfloat16), *...  9.87 us
    pallas_call x10, Pallas kernels, small_call(): pl.pallas_call(kernel, out_shape=shapes[0] if single else shapes, in_spec...  9.47 us
  transfers between devices with their start and end apart: 11, of which 6 were waited for; matrix products, arithmetic and copies ran while one was open for 0% of the time, Pallas kernels for 1%

profile of v1, /device:TPU:1, one launch (start us, length us, event | category | flops | bytes accessed | tf_op | source)
XLA Modules:
  0.0 333.9 jit_solution(5302421638860587868)
XLA Ops:
  0.0 1.4 collective-permute-start.1
  1.4 0.5 collective-permute-start.2
  1.9 0.8 collective-permute-done.rx_h
  3.8 1.9 slice_norm_pack.1
  5.7 20.8 %all_to_all.80 = bf16[16,16,2048]{2,1,0:T(8,128)(2,1)S(1)} all-to-all(bf16[16,16,2048]{2,1,0:T(8,128)(2,1)S(1)} %get-tuple-element.50), channel_id=1, replica_groups=mesh['pipe'=8,'expert'=16] {'expert'}, dimensions={0} | all-to-all | bytes 2097152 | tf_op jit(solution)/shard_map/all_to_all | solution.py:382
  26.6 4.8 %load_expert_ffn.2 = (bf16[256,2048]{1,0:T(8,128)(2,1)S(1)}, bf16[2048,768]{1,0:T(8,128)(2,1)S(1)}, bf16[2048,768]{1,0:T(8,128)(2,1)S(1)}, bf16[768,2048]{1,0:T(8,128)(2,1)S(1)}) custom-call(s32[1]{0:T(128)} %bitcast.section_ref, bf16[256,2048]{1,0:T(8,128)(2,1)S(1)} %bitcast.28, ...), custom_call_target="tpu_custom_call", output_to_operand_aliasing={{1}: (2, {}), {2}: (3, {}), {3}: (4, {})} | custom-call | flops 2415919104 | bytes 11534336 | tf_op jit(solution)/shard_map/load_expert_ffn/pallas_call | solution.py:335
  31.4 16.9 %all_to_all.81.returned_ref = bf16[16,16,2048]{2,1,0:T(8,128)(2,1)S(1)} all-to-all(bf16[16,16,2048]{2,1,0:T(8,128)(2,1)S(1)} %bitcast.42), channel_id=1, replica_groups=mesh['pipe'=8,'expert'=16] {'expert'}, dimensions={0} | all-to-all | bytes 2097152 | tf_op jit(solution)/shard_map/all_to_all | solution.py:382
  48.3 1.0 mix_norm_pack.4
  49.3 16.1 %all_to_all.82 = bf16[16,16,2048]{2,1,0:T(8,128)(2,1)S(1)} all-to-all(bf16[16,16,2048]{2,1,0:T(8,128)(2,1)S(1)} %get-tuple-element.57), channel_id=1, replica_groups=mesh['pipe'=8,'expert'=16] {'expert'}, dimensions={0} | all-to-all | bytes 2097152 | tf_op jit(solution)/shard_map/all_to_all | solution.py:382
  65.4 5.1 %load_expert_ffn.3 = (bf16[256,2048]{1,0:T(8,128)(2,1)S(1)}, bf16[2048,768]{1,0:T(8,128)(2,1)S(1)}, bf16[2048,768]{1,0:T(8,128)(2,1)S(1)}, bf16[768,2048]{1,0:T(8,128)(2,1)S(1)}) custom-call(s32[1]{0:T(128)} %bitcast.section_ref, bf16[256,2048]{1,0:T(8,128)(2,1)S(1)} %bitcast.29, bf16[2048,768]{1,0:T(8,128)(2,1)} %bitcast.46, bf16[2048,768]{1,0:T(8,128)(2,1)} %bitcast.49, ...), custom_call_target="tpu_custom_call" | custom-call | flops 2415919104 | bytes 11534336 | tf_op jit(solution)/shard_map/load_expert_ffn/pallas_call | solution.py:335
  70.5 15.7 %all_to_all.83.returned_ref = bf16[16,16,2048]{2,1,0:T(8,128)(2,1)S(1)} all-to-all(bf16[16,16,2048]{2,1,0:T(8,128)(2,1)S(1)} %bitcast.43), channel_id=1, replica_groups=mesh['pipe'=8,'expert'=16] {'expert'}, dimensions={0} | all-to-all | bytes 2097152 | tf_op jit(solution)/shard_map/all_to_all | solution.py:382
  86.2 1.3 mix.3
  87.4 1.2 collective-permute-start.6
  88.6 5.2 %collective-permute-done.6.hidden_ref = bf16[4,16,2048]{2,1,0:T(8,128)(2,1)S(1)} collective-permute-done((bf16[4,16,2048]{2,1,0:T(8,128)(2,1)S(1)}, bf16[4,16,2048]{2,1,0:T(8,128)(2,1)S(1)}, u32[]{:S(2)}, u32[]{:S(2)}) %collective-permute-start.6) | collective-permute-done | bytes 262176 | tf_op jit(solution)/shard_map/ppermute | solution.py:434
  93.9 0.8 norm_pack.3
  94.7 14.7 %all_to_all.84 = bf16[16,16,2048]{2,1,0:T(8,128)(2,1)S(1)} all-to-all(bf16[16,16,2048]{2,1,0:T(8,128)(2,1)S(1)} %norm_pack.3), channel_id=1, replica_groups=mesh['pipe'=8,'expert'=16] {'expert'}, dimensions={0} | all-to-all | bytes 2097152 | tf_op jit(solution)/shard_map/all_to_all | solution.py:382
  109.4 2.6 expert_ffn.6
  112.0 14.5 %all_to_all.85.returned_ref = bf16[16,16,2048]{2,1,0:T(8,128)(2,1)S(1)} all-to-all(bf16[16,16,2048]{2,1,0:T(8,128)(2,1)S(1)} %bitcast.36), channel_id=1, replica_groups=mesh['pipe'=8,'expert'=16] {'expert'}, dimensions={0} | all-to-all | bytes 2097152 | tf_op jit(solution)/shard_map/all_to_all | solution.py:382
  126.5 1.0 mix_norm_pack.5
  127.4 14.5 %all_to_all.86 = bf16[16,16,2048]{2,1,0:T(8,128)(2,1)S(1)} all-to-all(bf16[16,16,2048]{2,1,0:T(8,128)(2,1)S(1)} %get-tuple-element.64), channel_id=1, replica_groups=mesh['pipe'=8,'expert'=16] {'expert'}, dimensions={0} | all-to-all | bytes 2097152 | tf_op jit(solution)/shard_map/all_to_all | solution.py:382
  141.9 2.6 expert_ffn.7
  144.5 14.5 %all_to_all.87.returned_ref = bf16[16,16,2048]{2,1,0:T(8,128)(2,1)S(1)} all-to-all(bf16[16,16,2048]{2,1,0:T(8,128)(2,1)S(1)} %bitcast.37), channel_id=1, replica_groups=mesh['pipe'=8,'expert'=16] {'expert'}, dimensions={0} | all-to-all | bytes 2097152 | tf_op jit(solution)/shard_map/all_to_all | solution.py:382
  159.0 0.7 mix.4
  159.8 1.3 collective-permute-start.8
  161.1 12.9 %collective-permute-done.8.refs_0_ = bf16[16,128]{1,0:T(8,128)(2,1)S(1)} collective-permute-done((bf16[16,128]{1,0:T(8,128)(2,1)S(1)}, bf16[16,128]{1,0:T(8,128)(2,1)S(1)}, u32[]{:S(2)}, u32[]{:S(2)}) %collective-permute-start.8) | collective-permute-done | bytes 4128 | tf_op jit(solution)/shard_map/ppermute | solution.py:437
  174.0 0.8 norm_pack.4
  174.8 14.6 %all_to_all.88 = bf16[16,16,2048]{2,1,0:T(8,128)(2,1)S(1)} all-to-all(bf16[16,16,2048]{2,1,0:T(8,128)(2,1)S(1)} %norm_pack.4), channel_id=1, replica_groups=mesh['pipe'=8,'expert'=16] {'expert'}, dimensions={0} | all-to-all | bytes 2097152 | tf_op jit(solution)/shard_map/all_to_all | solution.py:382
  189.4 2.7 expert_ffn.8
  192.1 14.5 %all_to_all.89.returned_ref = bf16[16,16,2048]{2,1,0:T(8,128)(2,1)S(1)} all-to-all(bf16[16,16,2048]{2,1,0:T(8,128)(2,1)S(1)} %bitcast.39), channel_id=1, replica_groups=mesh['pipe'=8,'expert'=16] {'expert'}, dimensions={0} | all-to-all | bytes 2097152 | tf_op jit(solution)/shard_map/all_to_all | solution.py:382
  206.6 1.0 mix_norm_pack.6
  207.5 14.5 %all_to_all.90 = bf16[16,16,2048]{2,1,0:T(8,128)(2,1)S(1)} all-to-all(bf16[16,16,2048]{2,1,0:T(8,128)(2,1)S(1)} %get-tuple-element.71), channel_id=1, replica_groups=mesh['pipe'=8,'expert'=16] {'expert'}, dimensions={0} | all-to-all | bytes 2097152 | tf_op jit(solution)/shard_map/all_to_all | solution.py:382
  222.0 2.6 expert_ffn.9
  224.7 14.5 %all_to_all.91.returned_ref = bf16[16,16,2048]{2,1,0:T(8,128)(2,1)S(1)} all-to-all(bf16[16,16,2048]{2,1,0:T(8,128)(2,1)S(1)} %bitcast.41), channel_id=1, replica_groups=mesh['pipe'=8,'expert'=16] {'expert'}, dimensions={0} | all-to-all | bytes 2097152 | tf_op jit(solution)/shard_map/all_to_all | solution.py:382
  239.1 1.3 mix.5
  240.4 5.1 %collective-permute-start.9 = (bf16[4,16,2048]{2,1,0:T(8,128)(2,1)S(1)}, bf16[4,16,2048]{2,1,0:T(8,128)(2,1)S(1)}, u32[]{:S(2)}, u32[]{:S(2)}) collective-permute-start(bf16[4,16,2048]{2,1,0:T(8,128)(2,1)S(1)} %get-tuple-element.72.refs_6_), channel_id=1, source_target_pairs={{0,32},{16,48},{32,64},{48,80},{64,96},{80,112},{96,0},{112,16},{1... | collective-permute-start | bytes 786440 | tf_op jit(solution)/shard_map/ppermute | solution.py:434
  245.5 5.8 %collective-permute-done.9.hidden_ref = bf16[4,16,2048]{2,1,0:T(8,128)(2,1)S(1)} collective-permute-done((bf16[4,16,2048]{2,1,0:T(8,128)(2,1)S(1)}, bf16[4,16,2048]{2,1,0:T(8,128)(2,1)S(1)}, u32[]{:S(2)}, u32[]{:S(2)}) %collective-permute-start.9) | collective-permute-done | bytes 262176 | tf_op jit(solution)/shard_map/ppermute | solution.py:434
  251.4 0.8 norm_pack.5
  252.2 14.5 %all_to_all.92 = bf16[16,16,2048]{2,1,0:T(8,128)(2,1)S(1)} all-to-all(bf16[16,16,2048]{2,1,0:T(8,128)(2,1)S(1)} %norm_pack.5), channel_id=1, replica_groups=mesh['pipe'=8,'expert'=16] {'expert'}, dimensions={0} | all-to-all | bytes 2097152 | tf_op jit(solution)/shard_map/all_to_all | solution.py:382
  266.6 2.6 expert_ffn.10
  269.2 14.5 %all_to_all.93.returned_ref = bf16[16,16,2048]{2,1,0:T(8,128)(2,1)S(1)} all-to-all(bf16[16,16,2048]{2,1,0:T(8,128)(2,1)S(1)} %bitcast.31), channel_id=1, replica_groups=mesh['pipe'=8,'expert'=16] {'expert'}, dimensions={0} | all-to-all | bytes 2097152 | tf_op jit(solution)/shard_map/all_to_all | solution.py:382
  283.7 1.0 mix_norm_pack.7
  284.7 14.9 %all_to_all.94 = bf16[16,16,2048]{2,1,0:T(8,128)(2,1)S(1)} all-to-all(bf16[16,16,2048]{2,1,0:T(8,128)(2,1)S(1)} %get-tuple-element.74), channel_id=1, replica_groups=mesh['pipe'=8,'expert'=16] {'expert'}, dimensions={0} | all-to-all | bytes 2097152 | tf_op jit(solution)/shard_map/all_to_all | solution.py:382
  299.5 2.6 expert_ffn.11
  302.2 14.7 %all_to_all.95.returned_ref = bf16[16,16,2048]{2,1,0:T(8,128)(2,1)S(1)} all-to-all(bf16[16,16,2048]{2,1,0:T(8,128)(2,1)S(1)} %bitcast.33), channel_id=1, replica_groups=mesh['pipe'=8,'expert'=16] {'expert'}, dimensions={0} | all-to-all | bytes 2097152 | tf_op jit(solution)/shard_map/all_to_all | solution.py:382
  316.9 0.8 mix_choose.1
  317.8 13.9 %collective-permute-start.10 = (bf16[4,16,2048]{2,1,0:T(8,128)(2,1)S(1)}, bf16[4,16,2048]{2,1,0:T(8,128)(2,1)S(1)}, u32[]{:S(2)}, u32[]{:S(2)}) collective-permute-start(bf16[4,16,2048]{2,1,0:T(8,128)(2,1)S(1)} %get-tuple-element.76), channel_id=1, source_target_pairs={{0,16},{16,0},{32,48},{48,32},{64,80},{80,64},{96,112},{112,96},{1... | collective-permute-start | bytes 786440 | tf_op jit(solution)/shard_map/ppermute | solution.py:399
  331.7 1.2 collective-permute-done.10.got_ref
  332.9 0.8 join_rows.1
  (11 shorter events, 1.1 us)
Async XLA Ops:
  0.0 3.0 collective-permute-start.1
  1.4 1.4 collective-permute-start
  1.4 1.5 collective-permute-start.2
  3.0 23.6 %collective-permute-start.3 = (bf16[2048,768]{1,0:T(8,128)(2,1)}, bf16[2048,768]{1,0:T(8,128)(2,1)S(1)}, u32[]{:S(2)}, u32[]{:S(2)}) collective-permute-start(bf16[2048,768]{1,0:T(8,128)(2,1)} %bitcast.44), channel_id=1, source_target_pairs={{0,16},{16,0},{32,48},{48,32},{64,80},{80,64},{96,112},{112,96},{1... | collective-permute-start | bytes 9437192 | tf_op jit(solution)/shard_map/ppermute | solution.py:399
  3.3 23.3 %collective-permute-start.4 = (bf16[2048,768]{1,0:T(8,128)(2,1)}, bf16[2048,768]{1,0:T(8,128)(2,1)}, u32[]{:S(2)}, u32[]{:S(2)}) collective-permute-start(bf16[2048,768]{1,0:T(8,128)(2,1)} %bitcast.47), channel_id=1, source_target_pairs={{0,16},{16,0},{32,48},{48,32},{64,80},{80,64},{96,112},{112,96},{1... | collective-permute-start | bytes 9437192 | tf_op jit(solution)/shard_map/ppermute | solution.py:399
  3.5 23.1 %collective-permute-start.5 = (bf16[768,2048]{1,0:T(8,128)(2,1)}, bf16[768,2048]{1,0:T(8,128)(2,1)}, u32[]{:S(2)}, u32[]{:S(2)}) collective-permute-start(bf16[768,2048]{1,0:T(8,128)(2,1)} %bitcast.50), channel_id=1, source_target_pairs={{0,16},{16,0},{32,48},{48,32},{64,80},{80,64},{96,112},{112,96},{1... | collective-permute-start | bytes 9437192 | tf_op jit(solution)/shard_map/ppermute | solution.py:399
  87.4 6.4 %collective-permute-start.6 = (bf16[4,16,2048]{2,1,0:T(8,128)(2,1)S(1)}, bf16[4,16,2048]{2,1,0:T(8,128)(2,1)S(1)}, u32[]{:S(2)}, u32[]{:S(2)}) collective-permute-start(bf16[4,16,2048]{2,1,0:T(8,128)(2,1)S(1)} %get-tuple-element.59.refs_4_), channel_id=1, source_target_pairs={{0,32},{16,48},{32,64},{48,80},{64,96},{80,112},{96,0},{112,16},{1... | collective-permute-start | bytes 786440 | tf_op jit(solution)/shard_map/ppermute | solution.py:434
  159.8 14.2 %collective-permute-start.7 = (bf16[4,16,2048]{2,1,0:T(8,128)(2,1)S(1)}, bf16[4,16,2048]{2,1,0:T(8,128)(2,1)S(1)}, u32[]{:S(2)}, u32[]{:S(2)}) collective-permute-start(bf16[4,16,2048]{2,1,0:T(8,128)(2,1)S(1)} %get-tuple-element.68.refs_5_), channel_id=1, source_target_pairs={{0,32},{16,48},{32,64},{48,80},{64,96},{80,112},{96,0},{112,16},{1... | collective-permute-start | bytes 786440 | tf_op jit(solution)/shard_map/ppermute | solution.py:434
  159.8 14.2 %collective-permute-start.8 = (bf16[16,128]{1,0:T(8,128)(2,1)S(1)}, bf16[16,128]{1,0:T(8,128)(2,1)S(1)}, u32[]{:S(2)}, u32[]{:S(2)}) collective-permute-start(bf16[16,128]{1,0:T(8,128)(2,1)S(1)} %get-tuple-element.69), channel_id=1, source_target_pairs={{0,16},{32,48},{64,80},{96,112},{1,17},{33,49},{65,81},{97,113},{2... | collective-permute-start | bytes 12296 | tf_op jit(solution)/shard_map/ppermute | solution.py:437
  240.4 11.0 %collective-permute-start.9 = (bf16[4,16,2048]{2,1,0:T(8,128)(2,1)S(1)}, bf16[4,16,2048]{2,1,0:T(8,128)(2,1)S(1)}, u32[]{:S(2)}, u32[]{:S(2)}) collective-permute-start(bf16[4,16,2048]{2,1,0:T(8,128)(2,1)S(1)} %get-tuple-element.72.refs_6_), channel_id=1, source_target_pairs={{0,32},{16,48},{32,64},{48,80},{64,96},{80,112},{96,0},{112,16},{1... | collective-permute-start | bytes 786440 | tf_op jit(solution)/shard_map/ppermute | solution.py:434
  317.8 15.1 %collective-permute-start.10 = (bf16[4,16,2048]{2,1,0:T(8,128)(2,1)S(1)}, bf16[4,16,2048]{2,1,0:T(8,128)(2,1)S(1)}, u32[]{:S(2)}, u32[]{:S(2)}) collective-permute-start(bf16[4,16,2048]{2,1,0:T(8,128)(2,1)S(1)} %get-tuple-element.76), channel_id=1, source_target_pairs={{0,16},{16,0},{32,48},{48,32},{64,80},{80,64},{96,112},{112,96},{1... | collective-permute-start | bytes 786440 | tf_op jit(solution)/shard_map/ppermute | solution.py:399

commit v2 on v1

--- a/solution.py
+++ b/solution.py
@@ -121,8 +121,8 @@
             pltpu.VMEM(slots, jnp.bfloat16),
             pltpu.VMEM((2, 1, width), jnp.float32),
             *[pltpu.VMEM(w.shape, w.dtype) for w in own],
-            jax.ShapeDtypeStruct(both, jnp.int32),
-            jax.ShapeDtypeStruct(both, jnp.float32),
+            pltpu.SMEM(both, jnp.int32),
+            pltpu.SMEM(both, jnp.float32),
         ),
         in_specs=[spec(pltpu.SMEM)] + [spec(pl.ANY)] * 3 + [spec(pltpu.HBM)] * 7,
         out_specs=(spec(pltpu.VMEM),) * 6 + (spec(pltpu.SMEM),) * 2,
@@ -156,8 +156,9 @@
     pack(table_ids(1, ids_ref), normed_ref, packed_ref)
 
 
-def leave_kernel(ids_ref, scores_ref, hidden_ref, returned_ref, out_ref, token_ref):
-    token_ref[...] = jnp.zeros_like(token_ref)
+def leave_kernel(ids_ref, scores_ref, hidden_ref, returned_ref, out_ref, *token_refs):
+    for token_ref in token_refs:
+        token_ref[...] = jnp.zeros_like(token_ref)
     for block in range(hidden_ref.shape[0]):
         out_ref[block] = mixed(1, ids_ref, scores_ref, hidden_ref, returned_ref, block)
 
@@ -282,39 +283,43 @@
 
 
 def first_ffn_kernel(
-    section_ref, x_ref, gi, ui, di, gb, ub, db, out_ref, gate_ref, up_ref, down_ref, active_v, gate_sum, up_sum, down_sum, sems
+    section_ref, x_ref, gi, ui, di, gx, ux, dx, out_ref, gate_ref, up_ref, down_ref, gate_next, up_next, down_next,
+    active_v, gate_sum, up_sum, down_sum, sems
 ):
-    targets = (gate_ref, up_ref, down_ref)
-
     @pl.when(core_of(section_ref) == 0)
     def _():
-        ffn_kernel(x_ref, *targets, out_ref, active_v)
+        copies = load_copies((gx, ux, dx), (gate_next, up_next, down_next), sems)
+        for copy in copies:
+            copy.start()
+        ffn_kernel(x_ref, gate_ref, up_ref, down_ref, out_ref, active_v)
+        for copy in copies:
+            copy.wait()
 
     @pl.when(core_of(section_ref) != 0)
     def _():
-        copies = load_copies((gb, ub, db), targets, sems)
-        for copy in copies:
-            copy.start()
-        streamed_ffn(x_ref, targets, out_ref, active_v, gate_sum, up_sum, down_sum, copies)
+        stream_and_run(x_ref, (gx, ux, dx), (gate_ref, up_ref, down_ref), out_ref, active_v,
+                       gate_sum, up_sum, down_sum, sems)
 
 
 def second_ffn_kernel(
-    section_ref, x_ref, ga, ua, da, gb, ub, db, out_ref, gate_ref, up_ref, down_ref, active_v, gate_sum, up_sum, down_sum, sems
+    section_ref, x_ref, gi, ui, di, g_h, u_h, d_h, out_ref, gate_ref, up_ref, down_ref,
+    active_v, gate_sum, up_sum, down_sum, sems
 ):
-    targets = (gate_ref, up_ref, down_ref)
-
     @pl.when(core_of(section_ref) == 0)
     def _():
-        for copy in load_copies((gb, ub, db), targets, sems):
-            copy.start()
+        ffn_kernel(x_ref, gate_ref, up_ref, down_ref, out_ref, active_v)
 
     @pl.when(core_of(section_ref) != 0)
     def _():
-        for copy in load_copies((ga, ua, da), targets, sems):
-            copy.start()
-
-    waits = load_copies((ga, ua, da), targets, sems)
-    streamed_ffn(x_ref, targets, out_ref, active_v, gate_sum, up_sum, down_sum, waits)
+        stream_and_run(x_ref, (g_h, u_h, d_h), (gate_ref, up_ref, down_ref), out_ref, active_v,
+                       gate_sum, up_sum, down_sum, sems)
+
+
+def stream_and_run(x_ref, sources, targets, out_ref, active_v, gate_sum, up_sum, down_sum, sems):
+    copies = load_copies(sources, targets, sems)
+    for copy in copies:
+        copy.start()
+    streamed_ffn(x_ref, targets, out_ref, active_v, gate_sum, up_sum, down_sum, copies)
 
 
 def ffn_cost(flat, hidden):
@@ -326,17 +331,19 @@
     )
 
 
-def load_ffn(kernel, section_table, received, first, second, aliases):
+def load_ffn(kernel, section_table, received, present, sources, extra):
     experts, rows, width = received.shape
-    hidden = first[0].shape[1]
+    hidden = present[0].shape[1]
     flat = received.reshape(experts * rows, width)
     sums = pltpu.VMEM((flat.shape[0], hidden), jnp.float32)
-    place, kind = (in_vmem, pltpu.VMEM) if aliases else (in_hbm, pltpu.HBM)
     produced, *weights = pl.pallas_call(
         kernel,
-        out_shape=(pltpu.VMEM(flat.shape, jnp.bfloat16), *[pltpu.VMEM(w.shape, w.dtype) for w in first]),
-        in_specs=[spec(pltpu.SMEM), spec(pltpu.VMEM)] + [spec(kind)] * 3 + [spec(pl.ANY)] * 3,
-        out_specs=(spec(pltpu.VMEM),) * 4,
+        out_shape=(
+            pltpu.VMEM(flat.shape, jnp.bfloat16),
+            *[pltpu.VMEM(w.shape, w.dtype) for w in present] * (1 + extra),
+        ),
+        in_specs=[spec(pltpu.SMEM)] + [spec(pltpu.VMEM)] * 4 + [spec(pl.ANY if extra else pltpu.HBM)] * 3,
+        out_specs=(spec(pltpu.VMEM),) * (4 + 3 * extra),
         scratch_shapes=[
             pltpu.VMEM((flat.shape[0], hidden), jnp.bfloat16),
             sums,
@@ -344,11 +351,16 @@
             pltpu.VMEM(flat.shape, jnp.float32),
             pltpu.SemaphoreType.DMA((2 * (width // K_CUT) + DOWN_PARTS,)),
         ],
-        input_output_aliases=aliases,
+        input_output_aliases={2: 1, 3: 2, 4: 3},
         compiler_params=SMALL,
         cost_estimate=ffn_cost(flat, hidden),
         name="load_expert_ffn",
-    )(section_table, in_vmem(flat), *[place(w) for w in first], *second)
+    )(
+        section_table,
+        in_vmem(flat),
+        *[in_vmem(w) for w in present],
+        *(sources if extra else [in_hbm(w) for w in sources]),
+    )
     return produced.reshape(received.shape), weights
 
 
@@ -413,9 +425,8 @@
     out_a, out_b = [], []
     for step in range(stages):
         if step == 0:
-            made, weights_a = load_ffn(
-                first_ffn_kernel, section_table, exchange(sent), weights_a, other, {2: 1, 3: 2, 4: 3}
-            )
+            made, weights = load_ffn(first_ffn_kernel, section_table, exchange(sent), weights_a, other, 1)
+            weights_a, weights_b = weights[:3], weights[3:]
         else:
             made = ffn(exchange(sent), weights_a)
         hidden, sent = small_call(
@@ -423,18 +434,18 @@
         )
         out_a.append(hidden)
         if step == 0:
-            made, weights_b = load_ffn(second_ffn_kernel, section_table, exchange(sent), own, other, {})
+            made, weights_b = load_ffn(second_ffn_kernel, section_table, exchange(sent), weights_b, own, 0)
         else:
             made = ffn(exchange(sent), weights_b)
         back = exchange(made)
         if step == stages - 1:
             break
-        hidden, token = small_call(leave_kernel, "mix", (held, (16, 128)), (), (ids, scores), (hidden, back))
+        outs = (held, (16, 128)) if step in HELD else (held,)
+        left = small_call(leave_kernel, "mix", outs, (), (ids, scores), (hidden, back))
+        hidden, tokens = (left[0], left[1:]) if step in HELD else (left, ())
         out_b.append(hidden)
         hidden = lax.ppermute(hidden, "pipe", [(i, (i + 2) % sections) for i in range(sections)])
-        tokens = ()
-        if step in HELD:
-            tokens = (lax.ppermute(token, "pipe", [(i, i + 1) for i in range(0, sections, 2)]),)
+        tokens = [lax.ppermute(t, "pipe", [(i, i + 1) for i in range(0, sections, 2)]) for t in tokens]
         sent = small_call(enter_kernel, "norm_pack", (slots,), (held,), (ids,), (hidden, gains, *tokens))
 
     kept, leaving = finish(section_table, ids, scores, hidden, back, out_a + out_b)

time: 335 us -> 327 us (0.976)
  Pallas kernels: 38.8 us -> 30.6 us
    pallas_call x10, Pallas kernels: 9.47 us -> 2.57 us  [small_call(): pl.pallas_call(kernel, out_shape=shapes[0] if single else shapes, in_spec...]
  transfers between devices with their start and end apart: 11 -> 11, of which waited for: 6 -> 6; matrix products, arithmetic and copies ran while one was open for 0% -> 0% of each run, Pallas kernels for 1% -> 0%
where the time goes in v2:
time: 327 us; the launch traced here: 326 us
  blocking collectives  246 us (75%)
  Pallas kernels  30.6 us (9%)
  starting transfers between devices  24.8 us (8%)
  waiting for transfers between devices  24.2 us (7%)
    all_to_all x16, blocking collectives, exchange(): return lax.all_to_all(slots, 'expert', 0, 0, tiled=True)  246 us
    ppermute x7, starting transfers between devices, swapped(): return lax.ppermute(x, 'pipe', swap)  17 us
    pallas_call x6, Pallas kernels, ffn(): pl.pallas_call(ffn_kernel, out_shape=pltpu.VMEM(flat.shape, jnp.bfloat16)...  15.9 us
    ppermute x1, waiting for transfers between devices, shards(): lax.ppermute(t, 'pipe', [(i, i + 1) for i in range(0, sections, 2)])  11.2 us
    ppermute x3, waiting for transfers between devices, shards(): lax.ppermute(hidden, 'pipe', [(i, (i + 2) % sections) for i in range(sect...  10.8 us
    pallas_call x2, Pallas kernels, load_ffn(): pl.pallas_call(kernel, out_shape=(pltpu.VMEM(flat.shape, jnp.bfloat16), *...  9.87 us
    ppermute x3, starting transfers between devices, shards(): lax.ppermute(hidden, 'pipe', [(i, (i + 2) % sections) for i in range(sect...  6.57 us
  transfers between devices with their start and end apart: 11, of which 6 were waited for; matrix products, arithmetic and copies ran while one was open for 0% of the time, Pallas kernels for 0%

profile of v2, /device:TPU:1, one launch (start us, length us, event | category | flops | bytes accessed | tf_op | source)
XLA Modules:
  0.0 326.2 jit_solution(18191717459877743518)
XLA Ops:
  0.0 1.4 collective-permute-start.1
  1.4 0.5 collective-permute-start.2
  1.9 0.8 collective-permute-done.rx_h
  2.8 0.2 collective-permute-done.2.sx_h
  3.0 0.3 collective-permute-start.3
  3.5 0.3 collective-permute-start.5
  3.8 1.3 slice_norm_pack.1
  5.1 20.8 %all_to_all.80 = bf16[16,16,2048]{2,1,0:T(8,128)(2,1)S(1)} all-to-all(bf16[16,16,2048]{2,1,0:T(8,128)(2,1)S(1)} %get-tuple-element.51), channel_id=1, replica_groups=mesh['pipe'=8,'expert'=16] {'expert'}, dimensions={0} | all-to-all | bytes 2097152 | tf_op jit(solution)/shard_map/all_to_all | solution.py:394
  25.9 4.8 %load_expert_ffn.2 = (bf16[256,2048]{1,0:T(8,128)(2,1)S(1)}, bf16[2048,768]{1,0:T(8,128)(2,1)S(1)}, bf16[2048,768]{1,0:T(8,128)(2,1)S(1)}, bf16[768,2048]{1,0:T(...) custom-call(s32[1]{0:T(128)} %bitcast.section_ref, ...), custom_call_target="tpu_custom_call", output_to_operand_aliasing={{1}: (2, {}), {2}: (3, {}), {3}: (4, {})} | custom-call | flops 2415919104 | bytes 11534336 | tf_op jit(solution)/shard_map/load_expert_ffn/pallas_call | solution.py:339
  30.7 16.6 %all_to_all.81.returned_ref = bf16[16,16,2048]{2,1,0:T(8,128)(2,1)S(1)} all-to-all(bf16[16,16,2048]{2,1,0:T(8,128)(2,1)S(1)} %bitcast.42), channel_id=1, replica_groups=mesh['pipe'=8,'expert'=16] {'expert'}, dimensions={0} | all-to-all | bytes 2097152 | tf_op jit(solution)/shard_map/all_to_all | solution.py:394
  47.3 0.4 mix_norm_pack.4
  47.6 16.0 %all_to_all.82 = bf16[16,16,2048]{2,1,0:T(8,128)(2,1)S(1)} all-to-all(bf16[16,16,2048]{2,1,0:T(8,128)(2,1)S(1)} %get-tuple-element.58), channel_id=1, replica_groups=mesh['pipe'=8,'expert'=16] {'expert'}, dimensions={0} | all-to-all | bytes 2097152 | tf_op jit(solution)/shard_map/all_to_all | solution.py:394
  63.7 5.1 %load_expert_ffn.3 = (bf16[256,2048]{1,0:T(8,128)(2,1)S(1)}, bf16[2048,768]{1,0:T(8,128)(2,1)S(1)}, bf16[2048,768]{1,0:T(8,128)(2,1)S(1)}, bf16[768,2048]{1,0:T(8,128)(2,1)S(1)}) custom-call(s32[1]{0:T(128)} %bitcast.section_ref, bf16[256,2048]{1,0:T(8,128)(2,1)S(1)} %bitcast.29, ...), custom_call_target="tpu_custom_call", output_to_operand_aliasing={{1}: (2, {}), {2}: (3, {}), {3}: (4, {})} | custom-call | flops 2415919104 | bytes 11534336 | tf_op jit(solution)/shard_map/load_expert_ffn/pallas_call | solution.py:339
  68.7 16.8 %all_to_all.83.returned_ref = bf16[16,16,2048]{2,1,0:T(8,128)(2,1)S(1)} all-to-all(bf16[16,16,2048]{2,1,0:T(8,128)(2,1)S(1)} %bitcast.43), channel_id=1, replica_groups=mesh['pipe'=8,'expert'=16] {'expert'}, dimensions={0} | all-to-all | bytes 2097152 | tf_op jit(solution)/shard_map/all_to_all | solution.py:394
  85.7 1.3 collective-permute-start.6
  87.0 5.2 %collective-permute-done.6.hidden_ref = bf16[4,16,2048]{2,1,0:T(8,128)(2,1)S(1)} collective-permute-done((bf16[4,16,2048]{2,1,0:T(8,128)(2,1)S(1)}, bf16[4,16,2048]{2,1,0:T(8,128)(2,1)S(1)}, u32[]{:S(2)}, u32[]{:S(2)}) %collective-permute-start.6) | collective-permute-done | bytes 262176 | tf_op jit(solution)/shard_map/ppermute | solution.py:447
  92.2 0.2 norm_pack.3
  92.4 15.2 %all_to_all.84 = bf16[16,16,2048]{2,1,0:T(8,128)(2,1)S(1)} all-to-all(bf16[16,16,2048]{2,1,0:T(8,128)(2,1)S(1)} %norm_pack.3), channel_id=1, replica_groups=mesh['pipe'=8,'expert'=16] {'expert'}, dimensions={0} | all-to-all | bytes 2097152 | tf_op jit(solution)/shard_map/all_to_all | solution.py:394
  107.7 2.6 expert_ffn.6
  110.3 14.5 %all_to_all.85.returned_ref = bf16[16,16,2048]{2,1,0:T(8,128)(2,1)S(1)} all-to-all(bf16[16,16,2048]{2,1,0:T(8,128)(2,1)S(1)} %bitcast.36), channel_id=1, replica_groups=mesh['pipe'=8,'expert'=16] {'expert'}, dimensions={0} | all-to-all | bytes 2097152 | tf_op jit(solution)/shard_map/all_to_all | solution.py:394
  124.8 0.4 mix_norm_pack.5
  125.2 14.5 %all_to_all.86 = bf16[16,16,2048]{2,1,0:T(8,128)(2,1)S(1)} all-to-all(bf16[16,16,2048]{2,1,0:T(8,128)(2,1)S(1)} %get-tuple-element.67), channel_id=1, replica_groups=mesh['pipe'=8,'expert'=16] {'expert'}, dimensions={0} | all-to-all | bytes 2097152 | tf_op jit(solution)/shard_map/all_to_all | solution.py:394
  139.7 2.6 expert_ffn.7
  142.3 14.5 %all_to_all.87.returned_ref = bf16[16,16,2048]{2,1,0:T(8,128)(2,1)S(1)} all-to-all(bf16[16,16,2048]{2,1,0:T(8,128)(2,1)S(1)} %bitcast.37), channel_id=1, replica_groups=mesh['pipe'=8,'expert'=16] {'expert'}, dimensions={0} | all-to-all | bytes 2097152 | tf_op jit(solution)/shard_map/all_to_all | solution.py:394
  157.0 1.3 collective-permute-start.8
  158.3 11.2 %collective-permute-done.8.refs_0_ = bf16[16,128]{1,0:T(8,128)(2,1)S(1)} collective-permute-done((bf16[16,128]{1,0:T(8,128)(2,1)S(1)}, bf16[16,128]{1,0:T(8,128)(2,1)S(1)}, u32[]{:S(2)}, u32[]{:S(2)}) %collective-permute-start.8) | collective-permute-done | bytes 4128 | tf_op jit(solution)/shard_map/ppermute | solution.py:448
  169.5 0.2 norm_pack.4
  169.7 14.6 %all_to_all.88 = bf16[16,16,2048]{2,1,0:T(8,128)(2,1)S(1)} all-to-all(bf16[16,16,2048]{2,1,0:T(8,128)(2,1)S(1)} %norm_pack.4), channel_id=1, replica_groups=mesh['pipe'=8,'expert'=16] {'expert'}, dimensions={0} | all-to-all | bytes 2097152 | tf_op jit(solution)/shard_map/all_to_all | solution.py:394
  184.3 2.6 expert_ffn.8
  187.0 14.5 %all_to_all.89.returned_ref = bf16[16,16,2048]{2,1,0:T(8,128)(2,1)S(1)} all-to-all(bf16[16,16,2048]{2,1,0:T(8,128)(2,1)S(1)} %bitcast.39), channel_id=1, replica_groups=mesh['pipe'=8,'expert'=16] {'expert'}, dimensions={0} | all-to-all | bytes 2097152 | tf_op jit(solution)/shard_map/all_to_all | solution.py:394
  201.5 0.4 mix_norm_pack.6
  201.8 14.5 %all_to_all.90 = bf16[16,16,2048]{2,1,0:T(8,128)(2,1)S(1)} all-to-all(bf16[16,16,2048]{2,1,0:T(8,128)(2,1)S(1)} %get-tuple-element.74), channel_id=1, replica_groups=mesh['pipe'=8,'expert'=16] {'expert'}, dimensions={0} | all-to-all | bytes 2097152 | tf_op jit(solution)/shard_map/all_to_all | solution.py:394
  216.3 2.6 expert_ffn.9
  219.0 14.5 %all_to_all.91.returned_ref = bf16[16,16,2048]{2,1,0:T(8,128)(2,1)S(1)} all-to-all(bf16[16,16,2048]{2,1,0:T(8,128)(2,1)S(1)} %bitcast.41), channel_id=1, replica_groups=mesh['pipe'=8,'expert'=16] {'expert'}, dimensions={0} | all-to-all | bytes 2097152 | tf_op jit(solution)/shard_map/all_to_all | solution.py:394
  233.6 5.2 %collective-permute-start.9 = (bf16[4,16,2048]{2,1,0:T(8,128)(2,1)S(1)}, bf16[4,16,2048]{2,1,0:T(8,128)(2,1)S(1)}, u32[]{:S(2)}, u32[]{:S(2)}) collective-permute-start(bf16[4,16,2048]{2,1,0:T(8,128)(2,1)S(1)} %mix.5.refs_6_), channel_id=1, source_target_pairs={{0,32},{16,48},{32,64},{48,80},{64,96},{80,112},{96,0},{112,16},{1... | collective-permute-start | bytes 786440 | tf_op jit(solution)/shard_map/ppermute | solution.py:447
  238.8 5.6 %collective-permute-done.9.hidden_ref = bf16[4,16,2048]{2,1,0:T(8,128)(2,1)S(1)} collective-permute-done((bf16[4,16,2048]{2,1,0:T(8,128)(2,1)S(1)}, bf16[4,16,2048]{2,1,0:T(8,128)(2,1)S(1)}, u32[]{:S(2)}, u32[]{:S(2)}) %collective-permute-start.9) | collective-permute-done | bytes 262176 | tf_op jit(solution)/shard_map/ppermute | solution.py:447
  244.4 0.2 norm_pack.5
  244.6 14.5 %all_to_all.92 = bf16[16,16,2048]{2,1,0:T(8,128)(2,1)S(1)} all-to-all(bf16[16,16,2048]{2,1,0:T(8,128)(2,1)S(1)} %norm_pack.5), channel_id=1, replica_groups=mesh['pipe'=8,'expert'=16] {'expert'}, dimensions={0} | all-to-all | bytes 2097152 | tf_op jit(solution)/shard_map/all_to_all | solution.py:394
  259.1 2.6 expert_ffn.10
  261.8 14.5 %all_to_all.93.returned_ref = bf16[16,16,2048]{2,1,0:T(8,128)(2,1)S(1)} all-to-all(bf16[16,16,2048]{2,1,0:T(8,128)(2,1)S(1)} %bitcast.31), channel_id=1, replica_groups=mesh['pipe'=8,'expert'=16] {'expert'}, dimensions={0} | all-to-all | bytes 2097152 | tf_op jit(solution)/shard_map/all_to_all | solution.py:394
  276.2 0.4 mix_norm_pack.7
  276.6 15.5 %all_to_all.94 = bf16[16,16,2048]{2,1,0:T(8,128)(2,1)S(1)} all-to-all(bf16[16,16,2048]{2,1,0:T(8,128)(2,1)S(1)} %get-tuple-element.76), channel_id=1, replica_groups=mesh['pipe'=8,'expert'=16] {'expert'}, dimensions={0} | all-to-all | bytes 2097152 | tf_op jit(solution)/shard_map/all_to_all | solution.py:394
  292.0 2.6 expert_ffn.11
  294.7 14.9 %all_to_all.95.returned_ref = bf16[16,16,2048]{2,1,0:T(8,128)(2,1)S(1)} all-to-all(bf16[16,16,2048]{2,1,0:T(8,128)(2,1)S(1)} %bitcast.33), channel_id=1, replica_groups=mesh['pipe'=8,'expert'=16] {'expert'}, dimensions={0} | all-to-all | bytes 2097152 | tf_op jit(solution)/shard_map/all_to_all | solution.py:394
  309.6 0.3 mix_choose.1
  309.9 14.2 %collective-permute-start.10 = (bf16[4,16,2048]{2,1,0:T(8,128)(2,1)S(1)}, bf16[4,16,2048]{2,1,0:T(8,128)(2,1)S(1)}, u32[]{:S(2)}, u32[]{:S(2)}) collective-permute-start(bf16[4,16,2048]{2,1,0:T(8,128)(2,1)S(1)} %get-tuple-element.78), channel_id=1, source_target_pairs={{0,16},{16,0},{32,48},{48,32},{64,80},{80,64},{96,112},{112,96},{1... | collective-permute-start | bytes 786440 | tf_op jit(solution)/shard_map/ppermute | solution.py:411
  324.1 1.2 collective-permute-done.10.got_ref
  325.2 0.8 join_rows.1
  (11 shorter events, 0.7 us)
Async XLA Ops:
  0.0 3.0 collective-permute-start.1
  1.4 1.4 collective-permute-start
  1.4 1.5 collective-permute-start.2
  3.0 22.9 %collective-permute-start.3 = (bf16[2048,768]{1,0:T(8,128)(2,1)}, bf16[2048,768]{1,0:T(8,128)(2,1)S(1)}, u32[]{:S(2)}, u32[]{:S(2)}) collective-permute-start(bf16[2048,768]{1,0:T(8,128)(2,1)} %bitcast.44), channel_id=1, source_target_pairs={{0,16},{16,0},{32,48},{48,32},{64,80},{80,64},{96,112},{112,96},{1... | collective-permute-start | bytes 9437192 | tf_op jit(solution)/shard_map/ppermute | solution.py:411
  3.3 22.6 %collective-permute-start.4 = (bf16[2048,768]{1,0:T(8,128)(2,1)}, bf16[2048,768]{1,0:T(8,128)(2,1)}, u32[]{:S(2)}, u32[]{:S(2)}) collective-permute-start(bf16[2048,768]{1,0:T(8,128)(2,1)} %bitcast.47), channel_id=1, source_target_pairs={{0,16},{16,0},{32,48},{48,32},{64,80},{80,64},{96,112},{112,96},{1... | collective-permute-start | bytes 9437192 | tf_op jit(solution)/shard_map/ppermute | solution.py:411
  3.5 22.4 %collective-permute-start.5 = (bf16[768,2048]{1,0:T(8,128)(2,1)}, bf16[768,2048]{1,0:T(8,128)(2,1)}, u32[]{:S(2)}, u32[]{:S(2)}) collective-permute-start(bf16[768,2048]{1,0:T(8,128)(2,1)} %bitcast.50), channel_id=1, source_target_pairs={{0,16},{16,0},{32,48},{48,32},{64,80},{80,64},{96,112},{112,96},{1... | collective-permute-start | bytes 9437192 | tf_op jit(solution)/shard_map/ppermute | solution.py:411
  85.7 6.5 %collective-permute-start.6 = (bf16[4,16,2048]{2,1,0:T(8,128)(2,1)S(1)}, bf16[4,16,2048]{2,1,0:T(8,128)(2,1)S(1)}, u32[]{:S(2)}, u32[]{:S(2)}) collective-permute-start(bf16[4,16,2048]{2,1,0:T(8,128)(2,1)S(1)} %mix.3.refs_4_), channel_id=1, source_target_pairs={{0,32},{16,48},{32,64},{48,80},{64,96},{80,112},{96,0},{112,16},{1... | collective-permute-start | bytes 786440 | tf_op jit(solution)/shard_map/ppermute | solution.py:447
  156.9 12.6 %collective-permute-start.7 = (bf16[4,16,2048]{2,1,0:T(8,128)(2,1)S(1)}, bf16[4,16,2048]{2,1,0:T(8,128)(2,1)S(1)}, u32[]{:S(2)}, u32[]{:S(2)}) collective-permute-start(bf16[4,16,2048]{2,1,0:T(8,128)(2,1)S(1)} %get-tuple-element.71.refs_5_), channel_id=1, source_target_pairs={{0,32},{16,48},{32,64},{48,80},{64,96},{80,112},{96,0},{112,16},{1... | collective-permute-start | bytes 786440 | tf_op jit(solution)/shard_map/ppermute | solution.py:447
  157.0 12.5 %collective-permute-start.8 = (bf16[16,128]{1,0:T(8,128)(2,1)S(1)}, bf16[16,128]{1,0:T(8,128)(2,1)S(1)}, u32[]{:S(2)}, u32[]{:S(2)}) collective-permute-start(bf16[16,128]{1,0:T(8,128)(2,1)S(1)} %get-tuple-element.72), channel_id=1, source_target_pairs={{0,16},{32,48},{64,80},{96,112},{1,17},{33,49},{65,81},{97,113},{2... | collective-permute-start | bytes 12296 | tf_op jit(solution)/shard_map/ppermute | solution.py:448
  233.6 10.8 %collective-permute-start.9 = (bf16[4,16,2048]{2,1,0:T(8,128)(2,1)S(1)}, bf16[4,16,2048]{2,1,0:T(8,128)(2,1)S(1)}, u32[]{:S(2)}, u32[]{:S(2)}) collective-permute-start(bf16[4,16,2048]{2,1,0:T(8,128)(2,1)S(1)} %mix.5.refs_6_), channel_id=1, source_target_pairs={{0,32},{16,48},{32,64},{48,80},{64,96},{80,112},{96,0},{112,16},{1... | collective-permute-start | bytes 786440 | tf_op jit(solution)/shard_map/ppermute | solution.py:447
  309.9 15.4 %collective-permute-start.10 = (bf16[4,16,2048]{2,1,0:T(8,128)(2,1)S(1)}, bf16[4,16,2048]{2,1,0:T(8,128)(2,1)S(1)}, u32[]{:S(2)}, u32[]{:S(2)}) collective-permute-start(bf16[4,16,2048]{2,1,0:T(8,128)(2,1)S(1)} %get-tuple-element.78), channel_id=1, source_target_pairs={{0,16},{16,0},{32,48},{48,32},{64,80},{80,64},{96,112},{112,96},{1... | collective-permute-start | bytes 786440 | tf_op jit(solution)/shard_map/ppermute | solution.py:411
